TPU v7x, 512 devices: a whole 4x8x8 slice. The times are simulated.
512 devices in a mesh: shot: 32 (over y, x_lo, core), slab: 16 (over z, x_hi).
Axes of the slice: x: 4 (x_hi: 2, x_lo: 2; x = x_hi * 2 + x_lo), y: 8, z: 8, core: 2. Of those that a mesh axis runs over, the one named last changes fastest.
Arguments:
- velocity: float32 [256, 256, 128], P('slab', 'shot'), may hold values from 1.5 to 4.5
- aperture_start: int32 [32], P('shot'), may hold values from 0 to 28, as said below
- aperture_count: int32 [32], P('shot'), may hold values from 1 to 4
- wave_prev: float32 [32, 256, 32, 128], P('shot', 'slab'), may hold values from -6 to 6
- wave_now: float32 [32, 256, 32, 128], P('shot', 'slab'), may hold values from -6 to 6
- adjoint_prev: float32 [32, 256, 32, 128], P('shot', 'slab'), may hold values from -6 to 6
- adjoint_now: float32 [32, 256, 32, 128], P('shot', 'slab'), may hold values from -6 to 6
- source_cells: int32 [32, 4, 3], P('shot'), may hold values from 0 to 255, as said below
- wavelet: float32 [32, 4, 4], P('shot'), may hold values from -6 to 6
- receiver_cells: int32 [32, 16, 3], P('shot'), may hold values from 0 to 255, as said below
- trace: float32 [32, 4, 16], P('shot'), may hold values from -6 to 6
Outputs:
- wave_final: float32 [32, 256, 32, 128], P('shot', 'slab')
- adjoint_final: float32 [32, 256, 32, 128], P('shot', 'slab')
- gradient: float32 [256, 256, 128], P('slab', 'shot')
Inputs may be any that keep to these rules, and one draw needn't show every extreme that they name: aperture_start[g] lies between g - 3 and g, and at most 28. `source_cells`: x below 256, window y below 8, z below 128. `receiver_cells`: x below 256, window y below 8, z below 128.
All inputs are finite; a program needn't handle non-finite values.
Results may differ from a plain program's by a relative error of at most 0.0003.
Values sent between devices are 32-bit elements; how exact they have to be, the bound alone decides.
A program may use at most 64 MiB of HBM per device.

v0:
```python
import jax
import jax.numpy as jnp
from jax import lax
from jax.sharding import PartitionSpec as P

STEPS = 4


stencil_weights = (-205.0 / 72.0, 8.0 / 5.0, -1.0 / 5.0, 8.0 / 315.0, -1.0 / 560.0)
time_step = 0.09


def passed_along(block, axis, distance):
    devices = range(lax.axis_size(axis))
    route = [(i - distance, i) for i in devices if i - distance in devices]
    return lax.ppermute(block, axis, route)


def padded_2(cells, sides, width):
    for axis, dim in sides:
        count = lax.axis_size(axis)
        ends = count - 1
        head = lax.slice_in_dim(cells, 0, width, axis=dim)
        tail = lax.slice_in_dim(cells, cells.shape[dim] - width, cells.shape[dim], axis=dim)
        cells = jnp.concatenate(
            [
                lax.ppermute(tail, axis, [(i, (i + 1) % count) for i in range(ends)]),
                cells,
                lax.ppermute(head, axis, [((i + 1) % count, i) for i in range(ends)]),
            ],
            axis=dim,
        )
    return cells


def stencil(padded):
    size_x = padded.shape[-3] - 8
    size_y = padded.shape[-2] - 8
    size_z = padded.shape[-1] - 8
    center = padded[..., 4 : 4 + size_x, 4 : 4 + size_y, 4 : 4 + size_z]
    total = 3.0 * stencil_weights[0] * center
    for k in range(1, 5):
        near = padded[..., 4 + k : 4 + k + size_x, 4 : 4 + size_y, 4 : 4 + size_z]
        near = near + padded[..., 4 - k : 4 - k + size_x, 4 : 4 + size_y, 4 : 4 + size_z]
        near = near + padded[..., 4 : 4 + size_x, 4 + k : 4 + k + size_y, 4 : 4 + size_z]
        near = near + padded[..., 4 : 4 + size_x, 4 - k : 4 - k + size_y, 4 : 4 + size_z]
        near = near + padded[..., 4 : 4 + size_x, 4 : 4 + size_y, 4 + k : 4 + k + size_z]
        near = near + padded[..., 4 : 4 + size_x, 4 : 4 + size_y, 4 - k : 4 - k + size_z]
        total = total + stencil_weights[k] * near
    return total


def inject(cells, amps, x_cells, rows, depth):
    along_x = (x_cells[:, None] == cells[None, :, 0]).astype(jnp.float32) * amps[None, :]
    along_y = (jnp.arange(rows)[:, None] == cells[None, :, 1]).astype(jnp.float32)
    along_z = (jnp.arange(depth)[:, None] == cells[None, :, 2]).astype(jnp.float32)
    return jnp.einsum("xs,ys,zs->xyz", along_x, along_y, along_z, precision=lax.Precision.HIGHEST)


def per_device(
    velocity,
    aperture_start,
    aperture_count,
    wave_prev,
    wave_now,
    adjoint_prev,
    adjoint_now,
    source_cells,
    wavelet,
    receiver_cells,
    trace,
):
    slab_cells, block_rows, depth_cells = velocity.shape
    window_rows = wave_now.shape[2]
    aperture = window_rows // block_rows
    spread_blocks = aperture - 1
    group_index = lax.axis_index("shot")
    start_block = aperture_start[0]
    live_count = aperture_count[0]
    pieces = []
    for offset in range(-spread_blocks, spread_blocks + 1):
        if offset == 0:
            pieces.append(velocity)
        else:
            pieces.append(passed_along(velocity, "shot", -offset))
    nearby = jnp.concatenate(pieces, axis=1)
    window = lax.dynamic_slice_in_dim(
        nearby, (start_block - group_index + spread_blocks) * block_rows, window_rows, 1
    )
    x_cells = lax.axis_index("slab") * slab_cells + jnp.arange(slab_cells)
    live = (jnp.arange(window_rows) < live_count * block_rows).astype(jnp.float32)[None, :, None]
    courant = window * window * (time_step * time_step)
    imaging = 2.0 * time_step * time_step * window
    w_prev = wave_prev[0] * live
    w_now = wave_now[0] * live
    j_prev = adjoint_prev[0] * live
    j_now = adjoint_now[0] * live
    grad = jnp.zeros((slab_cells, window_rows, depth_cells), jnp.float32)
    for step in range(STEPS):
        stacked = jnp.stack([w_now, j_now])
        haloed = padded_2(stacked, (("slab", 1),), 4)
        padded = jnp.pad(haloed, ((0, 0), (0, 0), (4, 4), (4, 4)))
        lapl = stencil(padded)
        grad = grad + imaging * j_now * lapl[0]
        w_next = (
            2.0 * w_now
            - w_prev
            + courant * lapl[0]
            + inject(source_cells[0], wavelet[0, step], x_cells, window_rows, depth_cells)
        ) * live
        j_next = (
            2.0 * j_now
            - j_prev
            + courant * lapl[1]
            + inject(receiver_cells[0], trace[0, step], x_cells, window_rows, depth_cells)
        ) * live
        w_prev, w_now = (w_now, w_next)
        j_prev, j_now = (j_now, j_next)
    buffer = jnp.zeros((slab_cells, (2 * spread_blocks + 1) * block_rows, depth_cells), jnp.float32)
    buffer = lax.dynamic_update_slice_in_dim(
        buffer, grad, (start_block - group_index + spread_blocks) * block_rows, 1
    )
    gradient = buffer[:, spread_blocks * block_rows : (spread_blocks + 1) * block_rows, :]
    for offset in range(-spread_blocks, spread_blocks + 1):
        if offset != 0:
            piece = buffer[
                :,
                (spread_blocks + offset) * block_rows : (spread_blocks + offset + 1) * block_rows,
                :,
            ]
            gradient = gradient + passed_along(piece, "shot", offset)
    return (w_now[None], j_now[None], gradient)


def solution(mesh):
    return jax.shard_map(
        per_device,
        mesh=mesh,
        in_specs=(
            P("slab", "shot", None),
            P("shot"),
            P("shot"),
            P("shot", "slab", None, None),
            P("shot", "slab", None, None),
            P("shot", "slab", None, None),
            P("shot", "slab", None, None),
            P("shot", None, None),
            P("shot", None, None),
            P("shot", None, None),
            P("shot", None, None),
        ),
        out_specs=(
            P("shot", "slab", None, None),
            P("shot", "slab", None, None),
            P("slab", "shot", None),
        ),
        check_vma=False,
    )
```

profile of v0, /device:TPU:289, one launch (start us, length us, event | category | flops | bytes accessed | tf_op | source)
XLA Modules:
  0.0 148.0 jit_solution(13292160993420907127)
XLA Ops:
  1.6 2.9 %collective-permute-start = (f32[16,8,128]{2,0,1:T(8,128)S(1)}, f32[16,8,128]{2,0,1:T(8,128)S(1)}, u32[]{:S(2)}, u32[]{:S(2)}) collective-permute-start(f32[16,8,128]{2,0,1:T(8,128)S(1)} %copy.33), channel_id=1, source_target_pairs={{0,48},{16,64},{32,80},{48,96},{64,112},{80,128},{96,144},{112,160... | collective-permute-start | bytes 196616 | tf_op jit(solution)/shard_map/ppermute | solution.py:16
  4.4 3.1 %collective-permute-start.1 = (f32[16,8,128]{2,0,1:T(8,128)S(1)}, f32[16,8,128]{2,0,1:T(8,128)S(1)}, u32[]{:S(2)}, u32[]{:S(2)}) collective-permute-start(f32[16,8,128]{2,0,1:T(8,128)S(1)} %copy.33), channel_id=1, source_target_pairs={{0,32},{16,48},{32,64},{48,80},{64,96},{80,112},{96,128},{112,144}... | collective-permute-start | bytes 196616 | tf_op jit(solution)/shard_map/ppermute | solution.py:16
  7.6 3.1 %collective-permute-start.2 = (f32[16,8,128]{2,0,1:T(8,128)S(1)}, f32[16,8,128]{2,0,1:T(8,128)S(1)}, u32[]{:S(2)}, u32[]{:S(2)}) collective-permute-start(f32[16,8,128]{2,0,1:T(8,128)S(1)} %copy.33), channel_id=1, source_target_pairs={{0,16},{16,32},{32,48},{48,64},{64,80},{80,96},{96,112},{112,128},... | collective-permute-start | bytes 196616 | tf_op jit(solution)/shard_map/ppermute | solution.py:16
  10.7 1.9 %collective-permute-start.3 = (f32[16,8,128]{2,0,1:T(8,128)S(1)}, f32[16,8,128]{2,0,1:T(8,128)S(1)}, u32[]{:S(2)}, u32[]{:S(2)}) collective-permute-start(f32[16,8,128]{2,0,1:T(8,128)S(1)} %copy.33), channel_id=1, source_target_pairs={{16,0},{32,16},{48,32},{64,48},{80,64},{96,80},{112,96},{128,112},... | collective-permute-start | bytes 196616 | tf_op jit(solution)/shard_map/ppermute | solution.py:16
  12.6 4.3 %collective-permute-start.4 = (f32[16,8,128]{2,0,1:T(8,128)S(1)}, f32[16,8,128]{2,0,1:T(8,128)S(1)}, u32[]{:S(2)}, u32[]{:S(2)}) collective-permute-start(f32[16,8,128]{2,0,1:T(8,128)S(1)} %copy.33), channel_id=1, source_target_pairs={{32,0},{48,16},{64,32},{80,48},{96,64},{112,80},{128,96},{144,112}... | collective-permute-start | bytes 196616 | tf_op jit(solution)/shard_map/ppermute | solution.py:16
  23.7 4.7 %collective-permute-start.5 = (f32[16,8,128]{2,0,1:T(8,128)S(1)}, f32[16,8,128]{2,0,1:T(8,128)S(1)}, u32[]{:S(2)}, u32[]{:S(2)}) collective-permute-start(f32[16,8,128]{2,0,1:T(8,128)S(1)} %copy.33), channel_id=1, source_target_pairs={{48,0},{64,16},{80,32},{96,48},{112,64},{128,80},{144,96},{160,112... | collective-permute-start | bytes 196616 | tf_op jit(solution)/shard_map/ppermute | solution.py:16
  28.5 3.7 %collective-permute-start.6 = (f32[2,4,32,128]{3,1,2,0:T(4,128)S(1)}, f32[2,4,32,128]{3,1,2,0:T(4,128)S(1)}, u32[]{:S(2)}, u32[]{:S(2)}) collective-permute-start(f32[2,4,32,128]{3,1,2,0:T(4,128)S(1)} %get-tuple-element.27), channel_id=1, source_target_pairs={{1,0},{2,1},{3,2},{4,3},{5,4},{6,5},{7,6},{8,7},{9,8},{10,9},{11,1... | collective-permute-start | bytes 393224 | tf_op jit(solution)/shard_map/ppermute | solution.py:29
  32.2 3.0 %collective-permute-start.7 = (f32[2,4,32,128]{3,1,2,0:T(4,128)S(1)}, f32[2,4,32,128]{3,1,2,0:T(4,128)S(1)}, u32[]{:S(2)}, u32[]{:S(2)}) collective-permute-start(f32[2,4,32,128]{3,1,2,0:T(4,128)S(1)} %get-tuple-element.26), channel_id=1, source_target_pairs={{0,1},{1,2},{2,3},{3,4},{4,5},{5,6},{6,7},{7,8},{8,9},{9,10},{10,1... | collective-permute-start | bytes 393224 | tf_op jit(solution)/shard_map/ppermute | solution.py:27
  36.5 5.9 %collective-permute-done.7 = f32[2,4,32,128]{3,1,2,0:T(4,128)S(1)} collective-permute-done((f32[2,4,32,128]{3,1,2,0:T(4,128)S(1)}, f32[2,4,32,128]{3,1,2,0:T(4,128)S(1)}, u32[]{:S(2)}, u32[]{:S(2)}) %collective-permute-start.7) | collective-permute-done | bytes 131104 | tf_op jit(solution)/shard_map/ppermute | solution.py:27
  44.2 5.2 %fusion.40 = f32[2,16,32,128]{3,1,2,0:T(8,128)} fusion(f32[1,16,32,128]{3,1,2,0:T(8,128)} %copy-done.4, f32[1,16,32,128]{3,1,2,0:T(8,128)S(1)} %get-tuple-element.53, f32[2,24,40,136]{3,1,2,0:T(8,128)S(1)} %select_maximum_fusion.9, f32[2,20,32,128]{3,1,2,0:T(8,128)} %get-tuple-element.25, f32[2,20,32,128]{3,1,2,0:T(8,128)S(1)} %get-tuple-element.24), kind=kLoop, calls=%fused_computation.92 | loop fusion | flops 3932160 | bytes 13631488 | tf_op jit(solution)/shard_map/add | solution.py:49
  49.3 1.6 %fusion.13 = f32[16,32,128]{2,0,1:T(8,128)S(1)} fusion(f32[2,16,32,128]{3,1,2,0:T(8,128)} %fusion.40, f32[1,16,32,128]{3,2,1,0:T(8,128)} %param.16, f32[1,16,32,128]{3,2,1,0:T(8,128)} %param.17, f32[16,16]{0,1:T(8,128)S(1)} %get-tuple-element.48, f32[16,32]{0,1:T(8,128)S(1)} %convert_bitcast_fusion, f32[32]{0:T(128)S(1)} %compare_convert_fusion, ...), kind=kOutput, calls=%fused_computation.37 | convolution fusion | flops 13248512 | bytes 1313988 | tf_op jit(solution)/shard_map/xs,ys,zs->xyz/dot_general | solution.py:57
  51.0 1.8 %fusion.7 = f32[16,32,128]{2,0,1:T(8,128)S(1)} fusion(f32[1,16,32,128]{3,2,1,0:T(8,128)} %param.14, f32[2,16,32,128]{3,1,2,0:T(8,128)} %fusion.40, f32[1,16,32,128]{3,2,1,0:T(8,128)} %param.15, f32[32]{0:T(128)S(1)} %compare_convert_fusion, f32[4,16]{1,0:T(4,128)} %get-tuple-element.52, f32[4,32]{0,1:T(8,128)S(1)} %convert_bitcast_fusion.1, ...), kind=kOutput, calls=%fused_computation.27 | convolution fusion | flops 3803648 | bytes 1311636 | tf_op jit(solution)/shard_map/xs,ys,zs->xyz/dot_general | solution.py:57
  52.9 2.8 %collective-permute-start.8 = (f32[2,4,32,128]{3,1,2,0:T(4,128)S(1)}, f32[2,4,32,128]{3,1,2,0:T(4,128)S(1)}, u32[]{:S(2)}, u32[]{:S(2)}) collective-permute-start(f32[2,4,32,128]{3,1,2,0:T(4,128)S(1)} %get-tuple-element.23), channel_id=1, source_target_pairs={{1,0},{2,1},{3,2},{4,3},{5,4},{6,5},{7,6},{8,7},{9,8},{10,9},{11,1... | collective-permute-start | bytes 393224 | tf_op jit(solution)/shard_map/ppermute | solution.py:29
  55.6 4.0 %collective-permute-start.9 = (f32[2,4,32,128]{3,1,2,0:T(4,128)S(1)}, f32[2,4,32,128]{3,1,2,0:T(4,128)S(1)}, u32[]{:S(2)}, u32[]{:S(2)}) collective-permute-start(f32[2,4,32,128]{3,1,2,0:T(4,128)S(1)} %get-tuple-element.22), channel_id=1, source_target_pairs={{0,1},{1,2},{2,3},{3,4},{4,5},{5,6},{6,7},{7,8},{8,9},{9,10},{10,1... | collective-permute-start | bytes 393224 | tf_op jit(solution)/shard_map/ppermute | solution.py:27
  61.2 4.3 %collective-permute-done.9 = f32[2,4,32,128]{3,1,2,0:T(4,128)S(1)} collective-permute-done((f32[2,4,32,128]{3,1,2,0:T(4,128)S(1)}, f32[2,4,32,128]{3,1,2,0:T(4,128)S(1)}, u32[]{:S(2)}, u32[]{:S(2)}) %collective-permute-start.9) | collective-permute-done | bytes 131104 | tf_op jit(solution)/shard_map/ppermute | solution.py:27
  67.6 5.9 %fusion.35 = f32[2,16,32,128]{3,1,2,0:T(8,128)} fusion(f32[1,16,32,128]{3,1,2,0:T(8,128)S(1)} %bitcast.238, f32[1,16,32,128]{3,1,2,0:T(8,128)S(1)} %bitcast.250, f32[2,24,40,136]{3,1,2,0:T(8,128)S(1)} %select_maximum_fusion.6, f32[2,20,32,128]{3,1,2,0:T(8,128)} %get-tuple-element.21, f32[2,20,32,128]{3,1,2,0:T(8,128)} %get-tuple-element.20), kind=kLoop, calls=%fused_computation.87 | loop fusion | flops 3932160 | bytes 13631488 | tf_op jit(solution)/shard_map/add | solution.py:49
  76.6 3.5 %collective-permute-start.10 = (f32[2,4,32,128]{3,1,2,0:T(4,128)S(1)}, f32[2,4,32,128]{3,1,2,0:T(4,128)S(1)}, u32[]{:S(2)}, u32[]{:S(2)}) collective-permute-start(f32[2,4,32,128]{3,1,2,0:T(4,128)S(1)} %get-tuple-element.19), channel_id=1, source_target_pairs={{1,0},{2,1},{3,2},{4,3},{5,4},{6,5},{7,6},{8,7},{9,8},{10,9},{11,1... | collective-permute-start | bytes 393224 | tf_op jit(solution)/shard_map/ppermute | solution.py:29
  80.1 3.5 %collective-permute-start.11 = (f32[2,4,32,128]{3,1,2,0:T(4,128)S(1)}, f32[2,4,32,128]{3,1,2,0:T(4,128)S(1)}, u32[]{:S(2)}, u32[]{:S(2)}) collective-permute-start(f32[2,4,32,128]{3,1,2,0:T(4,128)S(1)} %get-tuple-element.18), channel_id=1, source_target_pairs={{0,1},{1,2},{2,3},{3,4},{4,5},{5,6},{6,7},{7,8},{8,9},{9,10},{10,1... | collective-permute-start | bytes 393224 | tf_op jit(solution)/shard_map/ppermute | solution.py:27
  83.8 5.6 %collective-permute-done.11 = f32[2,4,32,128]{3,1,2,0:T(4,128)S(1)} collective-permute-done((f32[2,4,32,128]{3,1,2,0:T(4,128)S(1)}, f32[2,4,32,128]{3,1,2,0:T(4,128)S(1)}, u32[]{:S(2)}, u32[]{:S(2)}) %collective-permute-start.11) | collective-permute-done | bytes 131104 | tf_op jit(solution)/shard_map/ppermute | solution.py:27
  91.5 5.9 %fusion.30 = f32[2,16,32,128]{3,1,2,0:T(8,128)} fusion(f32[1,16,32,128]{3,1,2,0:T(8,128)S(1)} %bitcast.234, f32[1,16,32,128]{3,1,2,0:T(8,128)S(1)} %bitcast.246, f32[2,24,40,136]{3,1,2,0:T(8,128)S(1)} %select_maximum_fusion.3, f32[2,20,32,128]{3,1,2,0:T(8,128)} %get-tuple-element.17, f32[2,20,32,128]{3,1,2,0:T(8,128)} %get-tuple-element.16), kind=kLoop, calls=%fused_computation.82 | loop fusion | flops 3932160 | bytes 13631488 | tf_op jit(solution)/shard_map/add | solution.py:49
  100.3 4.0 %collective-permute-start.12 = (f32[2,4,32,128]{3,1,2,0:T(4,128)S(1)}, f32[2,4,32,128]{3,1,2,0:T(4,128)S(1)}, u32[]{:S(2)}, u32[]{:S(2)}) collective-permute-start(f32[2,4,32,128]{3,1,2,0:T(4,128)S(1)} %get-tuple-element.15), channel_id=1, source_target_pairs={{1,0},{2,1},{3,2},{4,3},{5,4},{6,5},{7,6},{8,7},{9,8},{10,9},{11,1... | collective-permute-start | bytes 393224 | tf_op jit(solution)/shard_map/ppermute | solution.py:29
  104.3 2.8 %collective-permute-start.13 = (f32[2,4,32,128]{3,1,2,0:T(4,128)S(1)}, f32[2,4,32,128]{3,1,2,0:T(4,128)S(1)}, u32[]{:S(2)}, u32[]{:S(2)}) collective-permute-start(f32[2,4,32,128]{3,1,2,0:T(4,128)S(1)} %get-tuple-element.14), channel_id=1, source_target_pairs={{0,1},{1,2},{2,3},{3,4},{4,5},{5,6},{6,7},{7,8},{8,9},{9,10},{10,1... | collective-permute-start | bytes 393224 | tf_op jit(solution)/shard_map/ppermute | solution.py:27
  107.5 6.1 %collective-permute-done.13 = f32[2,4,32,128]{3,1,2,0:T(4,128)S(1)} collective-permute-done((f32[2,4,32,128]{3,1,2,0:T(4,128)S(1)}, f32[2,4,32,128]{3,1,2,0:T(4,128)S(1)}, u32[]{:S(2)}, u32[]{:S(2)}) %collective-permute-start.13) | collective-permute-done | bytes 131104 | tf_op jit(solution)/shard_map/ppermute | solution.py:27
  115.7 6.0 %fusion.25 = f32[2,16,32,128]{3,1,2,0:T(8,128)} fusion(f32[1,16,32,128]{3,1,2,0:T(8,128)S(1)} %bitcast.242, f32[1,16,32,128]{3,1,2,0:T(8,128)} %bitcast.254, f32[2,24,40,136]{3,1,2,0:T(8,128)S(1)} %select_maximum_fusion, f32[2,20,32,128]{3,1,2,0:T(8,128)} %get-tuple-element.13, f32[2,20,32,128]{3,1,2,0:T(8,128)} %get-tuple-element.12), kind=kLoop, calls=%fused_computation.77 | loop fusion | flops 3932160 | bytes 13631488 | tf_op jit(solution)/shard_map/add | solution.py:49
  121.7 1.6 %multiply_add_fusion = f32[16,32,128]{2,0,1:T(8,128)S(1)} fusion(f32[16,32,128]{2,0,1:T(8,128)S(1)} %fusion.17, f32[16,32,128]{2,0,1:T(8,128)S(1)} %fusion.15, f32[16,32,128]{2,0,1:T(8,128)S(1)} %fusion.13, f32[2,16,32,128]{3,1,2,0:T(8,128)} %fusion.40, f32[2,16,32,128]{3,1,2,0:T(8,128)} %fusion.35, f32[2,16,32,128]{3,1,2,0:T(8,128)} %fusion.30, ...), kind=kLoop, calls=%fused_computation.217 | loop fusion | flops 851968 | bytes 2621572 | tf_op jit(solution)/shard_map/add | solution.py:104
  123.5 3.8 %collective-permute-start.14 = (f32[16,8,128]{2,1,0:T(8,128)S(1)}, f32[16,8,128]{2,1,0:T(8,128)S(1)}, u32[]{:S(2)}, u32[]{:S(2)}) collective-permute-start(f32[16,8,128]{2,1,0:T(8,128)S(1)} %get-tuple-element.28), channel_id=1, source_target_pairs={{48,0},{64,16},{80,32},{96,48},{112,64},{128,80},{144,96},{160,112... | collective-permute-start | bytes 196616 | tf_op jit(solution)/shard_map/ppermute | solution.py:16
  127.3 3.0 %collective-permute-start.15 = (f32[16,8,128]{2,1,0:T(8,128)S(1)}, f32[16,8,128]{2,1,0:T(8,128)S(1)}, u32[]{:S(2)}, u32[]{:S(2)}) collective-permute-start(f32[16,8,128]{2,1,0:T(8,128)S(1)} %get-tuple-element.33), channel_id=1, source_target_pairs={{32,0},{48,16},{64,32},{80,48},{96,64},{112,80},{128,96},{144,112}... | collective-permute-start | bytes 196616 | tf_op jit(solution)/shard_map/ppermute | solution.py:16
  130.3 1.9 %collective-permute-start.16 = (f32[16,8,128]{2,1,0:T(8,128)S(1)}, f32[16,8,128]{2,1,0:T(8,128)S(1)}, u32[]{:S(2)}, u32[]{:S(2)}) collective-permute-start(f32[16,8,128]{2,1,0:T(8,128)S(1)} %get-tuple-element.32), channel_id=1, source_target_pairs={{16,0},{32,16},{48,32},{64,48},{80,64},{96,80},{112,96},{128,112},... | collective-permute-start | bytes 196616 | tf_op jit(solution)/shard_map/ppermute | solution.py:16
  132.3 3.6 %collective-permute-start.17 = (f32[16,8,128]{2,1,0:T(8,128)S(1)}, f32[16,8,128]{2,1,0:T(8,128)S(1)}, u32[]{:S(2)}, u32[]{:S(2)}) collective-permute-start(f32[16,8,128]{2,1,0:T(8,128)S(1)} %get-tuple-element.31), channel_id=1, source_target_pairs={{0,16},{16,32},{32,48},{48,64},{64,80},{80,96},{96,112},{112,128},... | collective-permute-start | bytes 196616 | tf_op jit(solution)/shard_map/ppermute | solution.py:16
  135.9 3.3 %collective-permute-start.18 = (f32[16,8,128]{2,1,0:T(8,128)S(1)}, f32[16,8,128]{2,1,0:T(8,128)S(1)}, u32[]{:S(2)}, u32[]{:S(2)}) collective-permute-start(f32[16,8,128]{2,1,0:T(8,128)S(1)} %get-tuple-element.30), channel_id=1, source_target_pairs={{0,32},{16,48},{32,64},{48,80},{64,96},{80,112},{96,128},{112,144}... | collective-permute-start | bytes 196616 | tf_op jit(solution)/shard_map/ppermute | solution.py:16
  139.6 2.5 %collective-permute-start.19 = (f32[16,8,128]{2,1,0:T(8,128)S(1)}, f32[16,8,128]{2,1,0:T(8,128)S(1)}, u32[]{:S(2)}, u32[]{:S(2)}) collective-permute-start(f32[16,8,128]{2,1,0:T(8,128)S(1)} %get-tuple-element.29), channel_id=1, source_target_pairs={{0,48},{16,64},{32,80},{48,96},{64,112},{80,128},{96,144},{112,160... | collective-permute-start | bytes 196616 | tf_op jit(solution)/shard_map/ppermute | solution.py:16
  144.2 3.1 %collective-permute-done.19 = f32[16,8,128]{2,1,0:T(8,128)S(1)} collective-permute-done((f32[16,8,128]{2,1,0:T(8,128)S(1)}, f32[16,8,128]{2,1,0:T(8,128)S(1)}, u32[]{:S(2)}, u32[]{:S(2)}) %collective-permute-start.19) | collective-permute-done | bytes 65568 | tf_op jit(solution)/shard_map/ppermute | solution.py:16
  (82 shorter events, 26.8 us)
Async XLA Ops:
  0.6 34.7 %copy-start.8 = (f32[16,8,128]{2,1,0:T(8,128)S(1)}, f32[16,8,128]{2,1,0:T(8,128)}, u32[]{:S(2)}) copy-start(f32[16,8,128]{2,1,0:T(8,128)} %param.11) | copy-start | bytes 196612
  1.6 22.2 %collective-permute-start = (f32[16,8,128]{2,0,1:T(8,128)S(1)}, f32[16,8,128]{2,0,1:T(8,128)S(1)}, u32[]{:S(2)}, u32[]{:S(2)}) collective-permute-start(f32[16,8,128]{2,0,1:T(8,128)S(1)} %copy.33), channel_id=1, source_target_pairs={{0,48},{16,64},{32,80},{48,96},{64,112},{80,128},{96,144},{112,160... | collective-permute-start | bytes 196616 | tf_op jit(solution)/shard_map/ppermute | solution.py:16
  4.4 24.0 %collective-permute-start.1 = (f32[16,8,128]{2,0,1:T(8,128)S(1)}, f32[16,8,128]{2,0,1:T(8,128)S(1)}, u32[]{:S(2)}, u32[]{:S(2)}) collective-permute-start(f32[16,8,128]{2,0,1:T(8,128)S(1)} %copy.33), channel_id=1, source_target_pairs={{0,32},{16,48},{32,64},{48,80},{64,96},{80,112},{96,128},{112,144}... | collective-permute-start | bytes 196616 | tf_op jit(solution)/shard_map/ppermute | solution.py:16
  7.6 24.7 %collective-permute-start.2 = (f32[16,8,128]{2,0,1:T(8,128)S(1)}, f32[16,8,128]{2,0,1:T(8,128)S(1)}, u32[]{:S(2)}, u32[]{:S(2)}) collective-permute-start(f32[16,8,128]{2,0,1:T(8,128)S(1)} %copy.33), channel_id=1, source_target_pairs={{0,16},{16,32},{32,48},{48,64},{64,80},{80,96},{96,112},{112,128},... | collective-permute-start | bytes 196616 | tf_op jit(solution)/shard_map/ppermute | solution.py:16
  10.7 24.7 %collective-permute-start.3 = (f32[16,8,128]{2,0,1:T(8,128)S(1)}, f32[16,8,128]{2,0,1:T(8,128)S(1)}, u32[]{:S(2)}, u32[]{:S(2)}) collective-permute-start(f32[16,8,128]{2,0,1:T(8,128)S(1)} %copy.33), channel_id=1, source_target_pairs={{16,0},{32,16},{48,32},{64,48},{80,64},{96,80},{112,96},{128,112},... | collective-permute-start | bytes 196616 | tf_op jit(solution)/shard_map/ppermute | solution.py:16
  12.6 22.8 %collective-permute-start.4 = (f32[16,8,128]{2,0,1:T(8,128)S(1)}, f32[16,8,128]{2,0,1:T(8,128)S(1)}, u32[]{:S(2)}, u32[]{:S(2)}) collective-permute-start(f32[16,8,128]{2,0,1:T(8,128)S(1)} %copy.33), channel_id=1, source_target_pairs={{32,0},{48,16},{64,32},{80,48},{96,64},{112,80},{128,96},{144,112}... | collective-permute-start | bytes 196616 | tf_op jit(solution)/shard_map/ppermute | solution.py:16
  22.9 20.5 %copy-start.4 = (f32[1,16,32,128]{3,1,2,0:T(8,128)}, f32[1,16,32,128]{3,1,2,0:T(8,128)S(1)}, u32[]{:S(2)}) copy-start(f32[1,16,32,128]{3,1,2,0:T(8,128)S(1)} %get-tuple-element.54) | copy-start | bytes 786436
  23.7 11.7 %collective-permute-start.5 = (f32[16,8,128]{2,0,1:T(8,128)S(1)}, f32[16,8,128]{2,0,1:T(8,128)S(1)}, u32[]{:S(2)}, u32[]{:S(2)}) collective-permute-start(f32[16,8,128]{2,0,1:T(8,128)S(1)} %copy.33), channel_id=1, source_target_pairs={{48,0},{64,16},{80,32},{96,48},{112,64},{128,80},{144,96},{160,112... | collective-permute-start | bytes 196616 | tf_op jit(solution)/shard_map/ppermute | solution.py:16
  28.5 8.1 %collective-permute-start.6 = (f32[2,4,32,128]{3,1,2,0:T(4,128)S(1)}, f32[2,4,32,128]{3,1,2,0:T(4,128)S(1)}, u32[]{:S(2)}, u32[]{:S(2)}) collective-permute-start(f32[2,4,32,128]{3,1,2,0:T(4,128)S(1)} %get-tuple-element.27), channel_id=1, source_target_pairs={{1,0},{2,1},{3,2},{4,3},{5,4},{6,5},{7,6},{8,7},{9,8},{10,9},{11,1... | collective-permute-start | bytes 393224 | tf_op jit(solution)/shard_map/ppermute | solution.py:29
  32.2 10.1 %collective-permute-start.7 = (f32[2,4,32,128]{3,1,2,0:T(4,128)S(1)}, f32[2,4,32,128]{3,1,2,0:T(4,128)S(1)}, u32[]{:S(2)}, u32[]{:S(2)}) collective-permute-start(f32[2,4,32,128]{3,1,2,0:T(4,128)S(1)} %get-tuple-element.26), channel_id=1, source_target_pairs={{0,1},{1,2},{2,3},{3,4},{4,5},{5,6},{6,7},{7,8},{8,9},{9,10},{10,1... | collective-permute-start | bytes 393224 | tf_op jit(solution)/shard_map/ppermute | solution.py:27
  35.4 63.3 %copy-start = (f32[16,56,128]{2,0,1:T(8,128)}, f32[16,56,128]{2,0,1:T(8,128)S(1)}, u32[]{:S(2)}) copy-start(f32[16,56,128]{2,0,1:T(8,128)S(1)} %constant_dynamic-update-slice_fusion) | copy-start | bytes 1376260
  52.9 8.3 %collective-permute-start.8 = (f32[2,4,32,128]{3,1,2,0:T(4,128)S(1)}, f32[2,4,32,128]{3,1,2,0:T(4,128)S(1)}, u32[]{:S(2)}, u32[]{:S(2)}) collective-permute-start(f32[2,4,32,128]{3,1,2,0:T(4,128)S(1)} %get-tuple-element.23), channel_id=1, source_target_pairs={{1,0},{2,1},{3,2},{4,3},{5,4},{6,5},{7,6},{8,7},{9,8},{10,9},{11,1... | collective-permute-start | bytes 393224 | tf_op jit(solution)/shard_map/ppermute | solution.py:29
  55.6 9.9 %collective-permute-start.9 = (f32[2,4,32,128]{3,1,2,0:T(4,128)S(1)}, f32[2,4,32,128]{3,1,2,0:T(4,128)S(1)}, u32[]{:S(2)}, u32[]{:S(2)}) collective-permute-start(f32[2,4,32,128]{3,1,2,0:T(4,128)S(1)} %get-tuple-element.22), channel_id=1, source_target_pairs={{0,1},{1,2},{2,3},{3,4},{4,5},{5,6},{6,7},{7,8},{8,9},{9,10},{10,1... | collective-permute-start | bytes 393224 | tf_op jit(solution)/shard_map/ppermute | solution.py:27
  67.6 6.0 %copy-start.5 = (f32[1,16,32,128]{3,2,1,0:T(8,128)S(1)}, f32[1,16,32,128]{3,2,1,0:T(8,128)}, u32[]{:S(2)}) copy-start(f32[1,16,32,128]{3,2,1,0:T(8,128)} %param.17) | copy-start | bytes 786436
  67.6 7.3 %copy-start.10 = (f32[4,16]{1,0:T(4,128)S(1)}, f32[4,16]{1,0:T(4,128)}, u32[]{:S(2)}) copy-start(f32[4,16]{1,0:T(4,128)} %get-tuple-element.51) | copy-start | bytes 772
  76.6 7.2 %collective-permute-start.10 = (f32[2,4,32,128]{3,1,2,0:T(4,128)S(1)}, f32[2,4,32,128]{3,1,2,0:T(4,128)S(1)}, u32[]{:S(2)}, u32[]{:S(2)}) collective-permute-start(f32[2,4,32,128]{3,1,2,0:T(4,128)S(1)} %get-tuple-element.19), channel_id=1, source_target_pairs={{1,0},{2,1},{3,2},{4,3},{5,4},{6,5},{7,6},{8,7},{9,8},{10,9},{11,1... | collective-permute-start | bytes 393224 | tf_op jit(solution)/shard_map/ppermute | solution.py:29
  80.1 9.3 %collective-permute-start.11 = (f32[2,4,32,128]{3,1,2,0:T(4,128)S(1)}, f32[2,4,32,128]{3,1,2,0:T(4,128)S(1)}, u32[]{:S(2)}, u32[]{:S(2)}) collective-permute-start(f32[2,4,32,128]{3,1,2,0:T(4,128)S(1)} %get-tuple-element.18), channel_id=1, source_target_pairs={{0,1},{1,2},{2,3},{3,4},{4,5},{5,6},{6,7},{7,8},{8,9},{9,10},{10,1... | collective-permute-start | bytes 393224 | tf_op jit(solution)/shard_map/ppermute | solution.py:27
  91.5 7.2 %copy-start.9 = (f32[4,16]{1,0:T(4,128)S(1)}, f32[4,16]{1,0:T(4,128)}, u32[]{:S(2)}) copy-start(f32[4,16]{1,0:T(4,128)} %get-tuple-element.50) | copy-start | bytes 772
  100.2 15.5 %copy-start.2 = (f32[16,32,128]{2,0,1:T(8,128)}, f32[16,32,128]{2,0,1:T(8,128)S(1)}, u32[]{:S(2)}) copy-start(f32[16,32,128]{2,0,1:T(8,128)S(1)} %fusion.9) | copy-start | bytes 786436
  100.3 7.2 %collective-permute-start.12 = (f32[2,4,32,128]{3,1,2,0:T(4,128)S(1)}, f32[2,4,32,128]{3,1,2,0:T(4,128)S(1)}, u32[]{:S(2)}, u32[]{:S(2)}) collective-permute-start(f32[2,4,32,128]{3,1,2,0:T(4,128)S(1)} %get-tuple-element.15), channel_id=1, source_target_pairs={{1,0},{2,1},{3,2},{4,3},{5,4},{6,5},{7,6},{8,7},{9,8},{10,9},{11,1... | collective-permute-start | bytes 393224 | tf_op jit(solution)/shard_map/ppermute | solution.py:29
  104.3 9.3 %collective-permute-start.13 = (f32[2,4,32,128]{3,1,2,0:T(4,128)S(1)}, f32[2,4,32,128]{3,1,2,0:T(4,128)S(1)}, u32[]{:S(2)}, u32[]{:S(2)}) collective-permute-start(f32[2,4,32,128]{3,1,2,0:T(4,128)S(1)} %get-tuple-element.14), channel_id=1, source_target_pairs={{0,1},{1,2},{2,3},{3,4},{4,5},{5,6},{6,7},{7,8},{8,9},{9,10},{10,1... | collective-permute-start | bytes 393224 | tf_op jit(solution)/shard_map/ppermute | solution.py:27
  115.7 6.0 %copy-start.6 = (f32[1,16,32,128]{3,2,1,0:T(8,128)S(1)}, f32[1,16,32,128]{3,2,1,0:T(8,128)}, u32[]{:S(2)}) copy-start(f32[1,16,32,128]{3,2,1,0:T(8,128)} %param.17) | copy-start | bytes 786436
  121.7 17.5 %copy-start.1 = (f32[16,56,128]{2,0,1:T(8,128)S(1)}, f32[16,56,128]{2,0,1:T(8,128)}, u32[]{:S(2)}) copy-start(f32[16,56,128]{2,0,1:T(8,128)} %copy-done) | copy-start | bytes 1376260
  121.7 17.5 %copy-start.7 = (f32[2,16,32,128]{3,1,2,0:T(8,128)S(1)}, f32[2,16,32,128]{3,1,2,0:T(8,128)}, u32[]{:S(2)}) copy-start(f32[2,16,32,128]{3,1,2,0:T(8,128)} %fusion.25) | copy-start | bytes 1572868
  123.3 18.7 %copy-start.3 = (f32[16,32,128]{2,0,1:T(8,128)S(1)}, f32[16,32,128]{2,0,1:T(8,128)}, u32[]{:S(2)}) copy-start(f32[16,32,128]{2,0,1:T(8,128)} %copy-done.2) | copy-start | bytes 786436
  123.5 16.1 %collective-permute-start.14 = (f32[16,8,128]{2,1,0:T(8,128)S(1)}, f32[16,8,128]{2,1,0:T(8,128)S(1)}, u32[]{:S(2)}, u32[]{:S(2)}) collective-permute-start(f32[16,8,128]{2,1,0:T(8,128)S(1)} %get-tuple-element.28), channel_id=1, source_target_pairs={{48,0},{64,16},{80,32},{96,48},{112,64},{128,80},{144,96},{160,112... | collective-permute-start | bytes 196616 | tf_op jit(solution)/shard_map/ppermute | solution.py:16
  127.3 16.8 %collective-permute-start.15 = (f32[16,8,128]{2,1,0:T(8,128)S(1)}, f32[16,8,128]{2,1,0:T(8,128)S(1)}, u32[]{:S(2)}, u32[]{:S(2)}) collective-permute-start(f32[16,8,128]{2,1,0:T(8,128)S(1)} %get-tuple-element.33), channel_id=1, source_target_pairs={{32,0},{48,16},{64,32},{80,48},{96,64},{112,80},{128,96},{144,112}... | collective-permute-start | bytes 196616 | tf_op jit(solution)/shard_map/ppermute | solution.py:16
  130.3 13.8 %collective-permute-start.16 = (f32[16,8,128]{2,1,0:T(8,128)S(1)}, f32[16,8,128]{2,1,0:T(8,128)S(1)}, u32[]{:S(2)}, u32[]{:S(2)}) collective-permute-start(f32[16,8,128]{2,1,0:T(8,128)S(1)} %get-tuple-element.32), channel_id=1, source_target_pairs={{16,0},{32,16},{48,32},{64,48},{80,64},{96,80},{112,96},{128,112},... | collective-permute-start | bytes 196616 | tf_op jit(solution)/shard_map/ppermute | solution.py:16
  132.3 11.9 %collective-permute-start.17 = (f32[16,8,128]{2,1,0:T(8,128)S(1)}, f32[16,8,128]{2,1,0:T(8,128)S(1)}, u32[]{:S(2)}, u32[]{:S(2)}) collective-permute-start(f32[16,8,128]{2,1,0:T(8,128)S(1)} %get-tuple-element.31), channel_id=1, source_target_pairs={{0,16},{16,32},{32,48},{48,64},{64,80},{80,96},{96,112},{112,128},... | collective-permute-start | bytes 196616 | tf_op jit(solution)/shard_map/ppermute | solution.py:16
  135.9 8.3 %collective-permute-start.18 = (f32[16,8,128]{2,1,0:T(8,128)S(1)}, f32[16,8,128]{2,1,0:T(8,128)S(1)}, u32[]{:S(2)}, u32[]{:S(2)}) collective-permute-start(f32[16,8,128]{2,1,0:T(8,128)S(1)} %get-tuple-element.30), channel_id=1, source_target_pairs={{0,32},{16,48},{32,64},{48,80},{64,96},{80,112},{96,128},{112,144}... | collective-permute-start | bytes 196616 | tf_op jit(solution)/shard_map/ppermute | solution.py:16
  139.6 7.7 %collective-permute-start.19 = (f32[16,8,128]{2,1,0:T(8,128)S(1)}, f32[16,8,128]{2,1,0:T(8,128)S(1)}, u32[]{:S(2)}, u32[]{:S(2)}) collective-permute-start(f32[16,8,128]{2,1,0:T(8,128)S(1)} %get-tuple-element.29), channel_id=1, source_target_pairs={{0,48},{16,64},{32,80},{48,96},{64,112},{80,128},{96,144},{112,160... | collective-permute-start | bytes 196616 | tf_op jit(solution)/shard_map/ppermute | solution.py:16
where the time goes:
time: 149 us; the launch traced here: 148 us
  starting transfers between devices  65.4 us (44%)
  other arithmetic  35.6 us (24%)
  waiting for transfers between devices  28.4 us (19%)
  matrix products  9.96 us (7%)
  local copies, waits for them, and re-layouts  6.1 us (4%)
  between operations  2.54 us (2%)
    ppermute x12, starting transfers between devices, passed_along(): return lax.ppermute(block, axis, route)  38.1 us
    add x4, other arithmetic, stencil(): total = total + stencil_weights[k] * near  23 us
    ppermute x4, waiting for transfers between devices, padded_2(): lax.ppermute(tail, axis, [(i, (i + 1) % count) for i in range(ends)])  21.9 us
    ppermute x4, starting transfers between devices, padded_2(): lax.ppermute(head, axis, [((i + 1) % count, i) for i in range(ends)])  14 us
    ppermute x4, starting transfers between devices, padded_2(): lax.ppermute(tail, axis, [(i, (i + 1) % count) for i in range(ends)])  13.3 us
    dot_general x8, matrix products, inject(): jnp.einsum('xs,ys,zs->xyz', along_x, along_y, along_z, precision=lax.Prec...  9.96 us
    concatenate x8, other arithmetic, padded_2(): jnp.concatenate([lax.ppermute(tail, axis, [(i, (i + 1) % count) for i in...  7.96 us
    unnamed x33, local copies, waits for them, and re-layouts  4.04 us
  transfers between devices with their start and end apart: 20, of which 9 were waited for; matrix products, arithmetic and copies ran while one was open for 5% of the time, Pallas kernels for 0%

commit v1 on v0

v1 whole, which is shorter than its diff:
```python
import functools

import jax
import jax.numpy as jnp
from jax import lax
from jax.experimental import pallas as pl
from jax.experimental.pallas import tpu as pltpu
from jax.sharding import PartitionSpec as P

MESH = pl.DeviceIdType.MESH
STEPS = 4
HALO = 4
PAD = 8
BLOCK = 4
REACH = 3

stencil_weights = (-205.0 / 72.0, 8.0 / 5.0, -1.0 / 5.0, 8.0 / 315.0, -1.0 / 560.0)
time_step = 0.09


def kernel(
    velocity,
    aperture_start,
    aperture_count,
    wave_prev,
    wave_now,
    adjoint_prev,
    adjoint_now,
    source_cells,
    wavelet,
    receiver_cells,
    trace,
    wave_out,
    adjoint_out,
    gradient_out,
    field,
    nearby,
    courant,
    imaging,
    grad,
    spread,
    injected,
    depth_op,
    to_sibling,
    from_sibling,
    to_far,
    from_far,
    to_pair,
    from_pair,
    own_grad,
    load_sem,
    store_sem,
    halo_send,
    halo_recv,
    block_send,
    block_recv,
    grad_send,
    grad_recv,
):
    layers, rows, depth = grad.shape
    brows = velocity.shape[1]
    blocks = rows // brows
    shots, slabs = lax.axis_size("shot"), lax.axis_size("slab")
    shot, slab = lax.axis_index("shot"), lax.axis_index("slab")
    core = lax.rem(shot, 2)
    sibling = shot + 1 - 2 * core
    far = shot - 3 + 6 * core
    has_left, has_right = slab > 0, slab < slabs - 1
    has_far = (far >= 0) & (far < shots)
    has_down, has_up = shot >= 2, shot < shots - 2
    inner = pl.ds(PAD, rows)
    mine = pl.ds(HALO, layers)

    def remote(src, dst, send, recv, where):
        return pltpu.make_async_remote_copy(
            src_ref=src, dst_ref=dst, send_sem=send, recv_sem=recv, device_id=where, device_id_type=MESH
        )

    left, right = {"slab": slab - 1}, {"slab": slab + 1}
    down, up = {"shot": shot - 2}, {"shot": shot + 2}
    partners = (
        (has_left, left),
        (has_right, right),
        (has_down, down),
        (has_up, up),
        (has_far, {"shot": far}),
        (None, {"shot": sibling}),
    )

    def on(condition, action):
        if condition is None:
            action()
        else:
            pl.when(condition)(action)

    loads = [
        pltpu.make_async_copy(wave_now.at[0], field.at[0, 1, mine, inner], load_sem.at[0]),
        pltpu.make_async_copy(adjoint_now.at[0], field.at[1, 1, mine, inner], load_sem.at[1]),
        pltpu.make_async_copy(wave_prev.at[0], field.at[0, 0, mine, inner], load_sem.at[2]),
        pltpu.make_async_copy(adjoint_prev.at[0], field.at[1, 0, mine, inner], load_sem.at[3]),
        pltpu.make_async_copy(velocity, nearby.at[REACH], load_sem.at[4]),
    ]
    for load in loads:
        load.start()

    def clear(edge):
        for f in range(2):
            for t in range(1, STEPS + 1):
                field[f, t, pl.ds(edge, HALO), inner, :] = jnp.zeros((HALO, rows, depth), jnp.float32)

    pl.when(jnp.logical_not(has_left))(lambda: clear(0))
    pl.when(jnp.logical_not(has_right))(lambda: clear(HALO + layers))

    barrier = pltpu.get_barrier_semaphore()
    for condition, where in partners:
        on(condition, lambda where=where: pl.semaphore_signal(barrier, inc=1, device_id=where, device_id_type=MESH))
    peers = 1
    for condition, _ in partners[:-1]:
        peers = peers + condition.astype(jnp.int32)
    pl.semaphore_wait(barrier, peers)

    def halo_copies(f, t, source):
        lo = source.at[pl.ds(0, HALO)] if t == 0 else field.at[f, t + 1, pl.ds(HALO, HALO), inner]
        hi = source.at[pl.ds(layers - HALO, HALO)] if t == 0 else field.at[f, t + 1, pl.ds(layers, HALO), inner]
        return (
            (has_left, has_right, remote(
                lo, field.at[f, t + 1, pl.ds(HALO + layers, HALO), inner],
                halo_send.at[f, t, 0], halo_recv.at[f, t, 0], left)),
            (has_right, has_left, remote(
                hi, field.at[f, t + 1, pl.ds(0, HALO), inner],
                halo_send.at[f, t, 1], halo_recv.at[f, t, 1], right)),
        )

    sources = (wave_now.at[0], adjoint_now.at[0])
    halos = [[halo_copies(f, t, sources[f]) for t in range(STEPS)] for f in range(2)]

    def start_halos(f, t):
        for to, _, copy in halos[f][t]:
            on(to, copy.start)

    def wait_halos(f, t):
        for _, given, copy in halos[f][t]:
            on(given, copy.wait_recv)

    shift = 2 * core - 1 + REACH
    velocity_far = (has_far, remote(
        velocity, nearby.at[6 * (1 - core)], block_send.at[0], block_recv.at[0], {"shot": far}))
    velocity_down = (has_down, has_up, remote(
        velocity, nearby.at[REACH + 2], block_send.at[1], block_recv.at[1], down))
    velocity_up = (has_up, has_down, remote(
        velocity, nearby.at[REACH - 2], block_send.at[2], block_recv.at[2], up))
    sibling_own = remote(velocity, nearby.at[shift], block_send.at[3], block_recv.at[3], {"shot": sibling})
    sibling_low = remote(
        nearby.at[REACH - 2], nearby.at[shift - 2], block_send.at[4], block_recv.at[4], {"shot": sibling})
    sibling_high = remote(
        nearby.at[REACH + 2], nearby.at[shift + 2], block_send.at[5], block_recv.at[5], {"shot": sibling})

    start_halos(0, 0)
    for send in (velocity_down, velocity_up, velocity_far):
        on(send[0], send[-1].start)
    sibling_own.start()
    start_halos(1, 0)

    def clear_rows(i, carry):
        for f in range(2):
            for t in range(1, STEPS + 1):
                field[f, t, HALO + i, pl.ds(0, PAD), :] = jnp.zeros((PAD, depth), jnp.float32)
                field[f, t, HALO + i, pl.ds(PAD + rows, PAD), :] = jnp.zeros((PAD, depth), jnp.float32)
        return carry

    lax.fori_loop(0, layers, clear_rows, 0)

    apart = jnp.abs(
        lax.broadcasted_iota(jnp.int32, (depth, depth), 0) - lax.broadcasted_iota(jnp.int32, (depth, depth), 1)
    )
    operator = jnp.zeros((depth, depth), jnp.float32)
    for k in range(1, HALO + 1):
        operator = jnp.where(apart == k, jnp.float32(stencil_weights[k]), operator)
    op_high = operator.astype(jnp.bfloat16)
    op_low = (operator - op_high.astype(jnp.float32)).astype(jnp.bfloat16)
    for half in range(2):
        depth_op[pl.ds(half * depth, depth), pl.ds(0, depth)] = op_high
        depth_op[pl.ds(half * depth, depth), pl.ds(depth, depth)] = op_low

    at_y = lax.broadcasted_iota(jnp.int32, (PAD, depth), 0)
    at_z = lax.broadcasted_iota(jnp.int32, (PAD, depth), 1)
    first = slab * layers
    for f, (cells, amps) in enumerate(((source_cells, wavelet), (receiver_cells, trace))):
        count = cells.shape[1]

        def inject(x, carry, f=f, cells=cells, amps=amps, count=count):
            sums = [jnp.zeros((PAD, depth), jnp.float32)] * STEPS
            for s in range(count):
                hit = (at_y == cells[0, s, 1]) & (at_z == cells[0, s, 2])
                here = cells[0, s, 0] == first + x
                for t in range(STEPS):
                    amp = jnp.where(here, amps[0, t, s], 0.0)
                    sums[t] = sums[t] + jnp.where(hit, amp, 0.0)
            for t in range(STEPS):
                injected[f, t, x] = sums[t]
            return carry

        lax.fori_loop(0, layers, inject, 0)

    live_rows = aperture_count[0] * brows
    at_row = lax.broadcasted_iota(jnp.int32, (1, rows, depth), 1)
    live = at_row < live_rows

    def keep(f, t, start, size):
        part = field[f, t, pl.ds(start, size), inner, :]
        field[f, t, pl.ds(start, size), inner, :] = jnp.where(live, part, 0.0)

    for i, (f, t) in enumerate(((0, 1), (1, 1), (0, 0), (1, 0))):
        loads[i].wait()
        lax.fori_loop(0, layers // BLOCK, lambda b, c, f=f, t=t: (keep(f, t, HALO + b * BLOCK, BLOCK), c)[1], 0)

    on(velocity_down[1], velocity_down[2].wait_recv)
    on(velocity_up[1], velocity_up[2].wait_recv)
    on(has_down, sibling_low.start)
    on(has_up, sibling_high.start)
    loads[4].wait()
    on(has_far, velocity_far[1].wait_recv)
    sibling_own.wait_recv()
    sib_down, sib_up = sibling >= 2, sibling < shots - 2
    on(sib_down, sibling_low.wait_recv)
    on(sib_up, sibling_high.wait_recv)

    offset = jnp.clip(aperture_start[0] - shot + REACH, 0, REACH)
    for j in range(blocks):
        part = nearby[offset + j]
        here = pl.ds(j * brows, brows)
        alive = j * brows < live_rows
        imaging[:, here, :] = part * jnp.float32(2.0 * time_step * time_step)
        courant[:, here, :] = jnp.where(alive, part * part * jnp.float32(time_step * time_step), 0.0)

    def advance(f, t, x):
        here = pl.ds(HALO + x, BLOCK)
        now = field[f, t + 1, here, inner, :]
        high = now.astype(jnp.bfloat16)
        low = (now - high.astype(jnp.float32)).astype(jnp.bfloat16)
        both = jnp.concatenate([high, low], axis=-1).reshape(BLOCK * rows, 2 * depth)
        along_z = jnp.dot(both, depth_op[...], preferred_element_type=jnp.float32)
        total = (along_z[:, :depth] + along_z[:, depth:]).reshape(BLOCK, rows, depth)
        total = total + jnp.float32(3.0 * stencil_weights[0]) * now
        for k in range(1, HALO + 1):
            near = field[f, t + 1, pl.ds(HALO + x + k, BLOCK), inner, :]
            near = near + field[f, t + 1, pl.ds(HALO + x - k, BLOCK), inner, :]
            near = near + field[f, t + 1, here, pl.ds(PAD + k, rows), :]
            near = near + field[f, t + 1, here, pl.ds(PAD - k, rows), :]
            total = total + jnp.float32(stencil_weights[k]) * near
        own = pl.ds(x, BLOCK)
        if f == 0:
            image = field[1, t + 1, here, inner, :] * total
            grad[own] = image if t == 0 else grad[own] + image
        later = 2.0 * now - field[f, t, here, inner, :] + courant[own] * total
        field[f, t + 2, here, pl.ds(PAD, PAD), :] = later[:, :PAD] + injected[f, t, own]
        field[f, t + 2, here, pl.ds(2 * PAD, rows - PAD), :] = later[:, PAD:]

    def inside(f, t):
        lax.fori_loop(1, layers // BLOCK - 1, lambda b, c: (advance(f, t, b * BLOCK), c)[1], 0)

    def edges(f, t):
        lax.fori_loop(0, 2, lambda b, c: (advance(f, t, b * (layers - BLOCK)), c)[1], 0)

    outs = [
        pltpu.make_async_copy(field.at[0, STEPS + 1, mine, inner], wave_out.at[0], store_sem.at[0]),
        pltpu.make_async_copy(field.at[1, STEPS + 1, mine, inner], adjoint_out.at[0], store_sem.at[1]),
        pltpu.make_async_copy(own_grad, gradient_out, store_sem.at[2]),
    ]

    grad_sibling = remote(to_sibling, from_sibling, grad_send.at[0], grad_recv.at[0], {"shot": sibling})
    grad_far = (has_far, remote(to_far, from_far, grad_send.at[1], grad_recv.at[1], {"shot": far}))
    grad_down = (has_down, has_up, remote(
        to_pair.at[0], from_pair.at[1], grad_send.at[2], grad_recv.at[2], down))
    grad_up = (has_up, has_down, remote(
        to_pair.at[1], from_pair.at[0], grad_send.at[3], grad_recv.at[3], up))
    back = 2 * REACH - offset

    def piece(o):
        return spread[back + o]

    def send_gradient():
        for j in range(REACH):
            spread[j] = jnp.zeros(spread.shape[1:], jnp.float32)
            spread[REACH + blocks + j] = jnp.zeros(spread.shape[1:], jnp.float32)
        for j in range(blocks):
            here = pl.ds(j * brows, brows)
            spread[REACH + j] = grad[:, here, :] * imaging[:, here, :]
        toward = 1 - 2 * core
        for i, o in enumerate((0, -2, 2)):
            to_sibling[i] = piece(toward + o)
        grad_sibling.start()
        to_far[...] = piece(6 * core - 3)
        on(has_far, grad_far[1].start)

    def pass_gradient():
        grad_sibling.wait_recv()
        to_pair[0] = piece(-2) + from_sibling[1]
        to_pair[1] = piece(2) + from_sibling[2]
        on(has_down, grad_down[2].start)
        on(has_up, grad_up[2].start)

    def take_gradient():
        total = piece(0) + from_sibling[0]
        on(has_far, grad_far[1].wait_recv)
        on(has_up, grad_down[2].wait_recv)
        on(has_down, grad_up[2].wait_recv)
        total = total + jnp.where(has_far, from_far[...], 0.0)
        total = total + jnp.where(has_down, from_pair[0], 0.0)
        total = total + jnp.where(has_up, from_pair[1], 0.0)
        own_grad[...] = total

    def mask_halos(f):
        keep(f, 1, 0, HALO)
        keep(f, 1, HALO + layers, HALO)

    for t in range(STEPS):
        last = t == STEPS - 1
        inside(0, t)
        wait_halos(0, t)
        if t == 0:
            mask_halos(0)
        edges(0, t)
        if last:
            outs[0].start()
            send_gradient()
        else:
            start_halos(0, t + 1)
        inside(1, t)
        if last:
            pass_gradient()
        wait_halos(1, t)
        if t == 0:
            mask_halos(1)
        edges(1, t)
        if last:
            outs[1].start()
        else:
            start_halos(1, t + 1)
    take_gradient()
    outs[2].start()

    for f in range(2):
        for t in range(STEPS):
            for to, _, copy in halos[f][t]:
                on(to, copy.wait_send)
    for send in (velocity_far, velocity_down, velocity_up, grad_far, grad_down, grad_up):
        on(send[0], send[-1].wait_send)
    sibling_own.wait_send()
    on(has_down, sibling_low.wait_send)
    on(has_up, sibling_high.wait_send)
    grad_sibling.wait_send()
    for out in outs:
        out.wait()


def per_device(*args):
    velocity, wave_now = args[0], args[4]
    layers, brows, depth = velocity.shape
    rows = wave_now.shape[2]
    blocks = rows // brows
    block = (layers, brows, depth)
    anywhere = pl.BlockSpec(memory_space=pl.ANY)
    scalars = pl.BlockSpec(memory_space=pltpu.SMEM)
    f32 = jnp.float32
    return pl.pallas_call(
        kernel,
        out_shape=(
            jax.ShapeDtypeStruct(wave_now.shape, f32),
            jax.ShapeDtypeStruct(wave_now.shape, f32),
            jax.ShapeDtypeStruct(velocity.shape, f32),
        ),
        in_specs=[anywhere, scalars, scalars] + [anywhere] * 4 + [scalars] * 4,
        out_specs=(anywhere,) * 3,
        scratch_shapes=[
            pltpu.VMEM((2, STEPS + 2, layers + 2 * HALO, rows + 2 * PAD, depth), f32),
            pltpu.VMEM((2 * REACH + 1, *block), f32),
            pltpu.VMEM((layers, rows, depth), f32),
            pltpu.VMEM((layers, rows, depth), f32),
            pltpu.VMEM((layers, rows, depth), f32),
            pltpu.VMEM((blocks + 2 * REACH, *block), f32),
            pltpu.VMEM((2, STEPS, layers, PAD, depth), f32),
            pltpu.VMEM((2 * depth, 2 * depth), jnp.bfloat16),
            pltpu.VMEM((3, *block), f32),
            pltpu.VMEM((3, *block), f32),
            pltpu.VMEM(block, f32),
            pltpu.VMEM(block, f32),
            pltpu.VMEM((2, *block), f32),
            pltpu.VMEM((2, *block), f32),
            pltpu.VMEM(block, f32),
            pltpu.SemaphoreType.DMA((5,)),
            pltpu.SemaphoreType.DMA((3,)),
            pltpu.SemaphoreType.DMA((2, STEPS, 2)),
            pltpu.SemaphoreType.DMA((2, STEPS, 2)),
            pltpu.SemaphoreType.DMA((6,)),
            pltpu.SemaphoreType.DMA((6,)),
            pltpu.SemaphoreType.DMA((4,)),
            pltpu.SemaphoreType.DMA((4,)),
        ],
        compiler_params=pltpu.CompilerParams(
            collective_id=0, has_side_effects=True, vmem_limit_bytes=60 * 1024 * 1024
        ),
        name="inversion",
    )(*args)


def solution(mesh):
    fields = P("shot", "slab", None, None)
    table = P("shot", None, None)
    return jax.shard_map(
        per_device,
        mesh=mesh,
        in_specs=(P("slab", "shot", None), P("shot"), P("shot"), fields, fields, fields, fields, table, table, table, table),
        out_specs=(fields, fields, P("slab", "shot", None)),
        check_vma=False,
    )
```

time: 149 us -> 51.7 us (0.35)
  the two profiles are of different devices: /device:TPU:289 before, /device:TPU:347 now
where the time goes in v1:
time: 51.7 us; the launch traced here: 51.4 us
  Pallas kernels  44.9 us (87%)
  local copies, waits for them, and re-layouts  4.57 us (9%)
  between operations  1.98 us (4%)
    pallas_call x1, Pallas kernels, per_device(): pl.pallas_call(kernel, out_shape=(jax.ShapeDtypeStruct(wave_now.shape, f3...  44.9 us
    unnamed x13, local copies, waits for them, and re-layouts  4.57 us

profile of v1, /device:TPU:347, one launch (start us, length us, event | category | flops | bytes accessed | tf_op | source)
XLA Modules:
  0.0 51.4 jit_solution(12898787935463322132)
XLA Ops:
  0.6 0.0 copy-start.2
  1.9 0.0 copy-done.2
  2.0 0.0 copy-start.3
  2.0 0.7 %copy.14.source_cells = s32[1,4,3]{2,1,0:T(4,128)} copy(s32[1,4,3]{1,0,2:T(1,128)S(1)} %copy-done.2) | data formatting | bytes 96 | tf_op args[7]
  2.6 0.0 copy-done.3
  2.6 0.7 %copy.15.receiver_cells = s32[1,16,3]{2,1,0:T(8,128)} copy(s32[1,16,3]{1,0,2:T(1,128)S(1)} %copy-done.3) | data formatting | bytes 384 | tf_op args[9]
  3.3 44.9 %inversion.1 = (f32[1,16,32,128]{3,2,1,0:T(8,128)}, f32[1,16,32,128]{3,2,1,0:T(8,128)}, f32[16,8,128]{2,1,0:T(8,128)}) custom-call(f32[16,8,128]{2,1,0:T(8,128)} %velocity.1, s32[1]{0:T(128)S(6)} %copy.19.aperture_start, s32[1]{0:T(128)S(6)} %copy.20.aperture_count, f32[1,16,32,128]{3,2,1,0:T(8,128)} %wave_prev.1, f32[1,16,32,128]{3,2,1,0:T(8,128)} %wave_now.1, ...), custom_call_target="tpu_custom_call" | custom-call | tf_op jit(solution)/shard_map/inversion/pallas_call | solution.py:366
  48.2 0.0 copy-start
  48.2 1.7 %copy.21 = f32[1,16,32,128]{3,2,1,0:T(8,128)} copy(f32[1,16,32,128]{3,2,1,0:T(8,128)} %get-tuple-element.6) | data formatting | bytes 524288
  49.9 0.0 copy-done
  49.9 0.0 copy-start.1
  49.9 0.7 %copy.22 = f32[1,16,32,128]{3,2,1,0:T(8,128)} copy(f32[1,16,32,128]{3,2,1,0:T(8,128)S(1)} %copy-done) | data formatting | bytes 524288
  50.6 0.2 copy-done.1
  50.8 0.6 %copy.23 = f32[16,8,128]{2,1,0:T(8,128)} copy(f32[16,8,128]{2,1,0:T(8,128)S(1)} %copy-done.1) | data formatting | bytes 131072
Async XLA Ops:
  0.6 1.3 %copy-start.2 = (s32[1,4,3]{1,0,2:T(1,128)S(1)}, s32[1,4,3]{1,0,2:T(1,128)}, u32[]{:S(2)}) copy-start(s32[1,4,3]{1,0,2:T(1,128)} %param.18) | copy-start | bytes 148
  2.0 0.7 %copy-start.3 = (s32[1,16,3]{1,0,2:T(1,128)S(1)}, s32[1,16,3]{1,0,2:T(1,128)}, u32[]{:S(2)}) copy-start(s32[1,16,3]{1,0,2:T(1,128)} %param.20) | copy-start | bytes 580
  48.2 1.7 %copy-start = (f32[1,16,32,128]{3,2,1,0:T(8,128)S(1)}, f32[1,16,32,128]{3,2,1,0:T(8,128)}, u32[]{:S(2)}) copy-start(f32[1,16,32,128]{3,2,1,0:T(8,128)} %get-tuple-element.7) | copy-start | bytes 786436
  49.9 0.9 %copy-start.1 = (f32[16,8,128]{2,1,0:T(8,128)S(1)}, f32[16,8,128]{2,1,0:T(8,128)}, u32[]{:S(2)}) copy-start(f32[16,8,128]{2,1,0:T(8,128)} %get-tuple-element.8) | copy-start | bytes 196612

commit v2 on v1

--- a/solution.py
+++ b/solution.py
@@ -47,9 +47,7 @@
     from_far,
     to_pair,
     from_pair,
-    own_grad,
     load_sem,
-    store_sem,
     halo_send,
     halo_recv,
     block_send,
@@ -186,13 +184,13 @@
     at_z = lax.broadcasted_iota(jnp.int32, (PAD, depth), 1)
     first = slab * layers
     for f, (cells, amps) in enumerate(((source_cells, wavelet), (receiver_cells, trace))):
-        count = cells.shape[1]
+        count = cells.shape[-1]
 
         def inject(x, carry, f=f, cells=cells, amps=amps, count=count):
             sums = [jnp.zeros((PAD, depth), jnp.float32)] * STEPS
             for s in range(count):
-                hit = (at_y == cells[0, s, 1]) & (at_z == cells[0, s, 2])
-                here = cells[0, s, 0] == first + x
+                hit = (at_y == cells[1, 0, s]) & (at_z == cells[2, 0, s])
+                here = cells[0, 0, s] == first + x
                 for t in range(STEPS):
                     amp = jnp.where(here, amps[0, t, s], 0.0)
                     sums[t] = sums[t] + jnp.where(hit, amp, 0.0)
@@ -249,24 +247,22 @@
             near = near + field[f, t + 1, here, pl.ds(PAD - k, rows), :]
             total = total + jnp.float32(stencil_weights[k]) * near
         own = pl.ds(x, BLOCK)
+        if t == STEPS - 1:
+            kept, at, row = (wave_out, adjoint_out)[f].at[0], own, 0
+        else:
+            kept, at, row = field.at[f, t + 2], here, PAD
         if f == 0:
             image = field[1, t + 1, here, inner, :] * total
             grad[own] = image if t == 0 else grad[own] + image
         later = 2.0 * now - field[f, t, here, inner, :] + courant[own] * total
-        field[f, t + 2, here, pl.ds(PAD, PAD), :] = later[:, :PAD] + injected[f, t, own]
-        field[f, t + 2, here, pl.ds(2 * PAD, rows - PAD), :] = later[:, PAD:]
+        kept[at, pl.ds(row, PAD), :] = later[:, :PAD] + injected[f, t, own]
+        kept[at, pl.ds(row + PAD, rows - PAD), :] = later[:, PAD:]
 
     def inside(f, t):
         lax.fori_loop(1, layers // BLOCK - 1, lambda b, c: (advance(f, t, b * BLOCK), c)[1], 0)
 
     def edges(f, t):
         lax.fori_loop(0, 2, lambda b, c: (advance(f, t, b * (layers - BLOCK)), c)[1], 0)
-
-    outs = [
-        pltpu.make_async_copy(field.at[0, STEPS + 1, mine, inner], wave_out.at[0], store_sem.at[0]),
-        pltpu.make_async_copy(field.at[1, STEPS + 1, mine, inner], adjoint_out.at[0], store_sem.at[1]),
-        pltpu.make_async_copy(own_grad, gradient_out, store_sem.at[2]),
-    ]
 
     grad_sibling = remote(to_sibling, from_sibling, grad_send.at[0], grad_recv.at[0], {"shot": sibling})
     grad_far = (has_far, remote(to_far, from_far, grad_send.at[1], grad_recv.at[1], {"shot": far}))
@@ -308,7 +304,7 @@
         total = total + jnp.where(has_far, from_far[...], 0.0)
         total = total + jnp.where(has_down, from_pair[0], 0.0)
         total = total + jnp.where(has_up, from_pair[1], 0.0)
-        own_grad[...] = total
+        gradient_out[...] = total
 
     def mask_halos(f):
         keep(f, 1, 0, HALO)
@@ -322,7 +318,6 @@
             mask_halos(0)
         edges(0, t)
         if last:
-            outs[0].start()
             send_gradient()
         else:
             start_halos(0, t + 1)
@@ -333,12 +328,9 @@
         if t == 0:
             mask_halos(1)
         edges(1, t)
-        if last:
-            outs[1].start()
-        else:
+        if not last:
             start_halos(1, t + 1)
     take_gradient()
-    outs[2].start()
 
     for f in range(2):
         for t in range(STEPS):
@@ -350,12 +342,31 @@
     on(has_down, sibling_low.wait_send)
     on(has_up, sibling_high.wait_send)
     grad_sibling.wait_send()
-    for out in outs:
-        out.wait()
-
-
-def per_device(*args):
-    velocity, wave_now = args[0], args[4]
+
+
+def deliver(*refs):
+    count = len(refs) // 2
+    done = refs[-1]
+    copies = [pltpu.make_async_copy(refs[i], refs[count + i], done.at[i]) for i in range(count)]
+    for copy in copies:
+        copy.start()
+    for copy in copies:
+        copy.wait()
+
+
+def per_device(
+    velocity,
+    aperture_start,
+    aperture_count,
+    wave_prev,
+    wave_now,
+    adjoint_prev,
+    adjoint_now,
+    source_cells,
+    wavelet,
+    receiver_cells,
+    trace,
+):
     layers, brows, depth = velocity.shape
     rows = wave_now.shape[2]
     blocks = rows // brows
@@ -363,17 +374,18 @@
     anywhere = pl.BlockSpec(memory_space=pl.ANY)
     scalars = pl.BlockSpec(memory_space=pltpu.SMEM)
     f32 = jnp.float32
-    return pl.pallas_call(
+    out_shape = (
+        jax.ShapeDtypeStruct(wave_now.shape, f32),
+        jax.ShapeDtypeStruct(wave_now.shape, f32),
+        jax.ShapeDtypeStruct(velocity.shape, f32),
+    )
+    results = pl.pallas_call(
         kernel,
-        out_shape=(
-            jax.ShapeDtypeStruct(wave_now.shape, f32),
-            jax.ShapeDtypeStruct(wave_now.shape, f32),
-            jax.ShapeDtypeStruct(velocity.shape, f32),
-        ),
+        out_shape=tuple(pltpu.VMEM(leaf.shape, leaf.dtype) for leaf in out_shape),
         in_specs=[anywhere, scalars, scalars] + [anywhere] * 4 + [scalars] * 4,
-        out_specs=(anywhere,) * 3,
+        out_specs=(pl.BlockSpec(memory_space=pltpu.VMEM),) * 3,
         scratch_shapes=[
-            pltpu.VMEM((2, STEPS + 2, layers + 2 * HALO, rows + 2 * PAD, depth), f32),
+            pltpu.VMEM((2, STEPS + 1, layers + 2 * HALO, rows + 2 * PAD, depth), f32),
             pltpu.VMEM((2 * REACH + 1, *block), f32),
             pltpu.VMEM((layers, rows, depth), f32),
             pltpu.VMEM((layers, rows, depth), f32),
@@ -387,9 +399,7 @@
             pltpu.VMEM(block, f32),
             pltpu.VMEM((2, *block), f32),
             pltpu.VMEM((2, *block), f32),
-            pltpu.VMEM(block, f32),
             pltpu.SemaphoreType.DMA((5,)),
-            pltpu.SemaphoreType.DMA((3,)),
             pltpu.SemaphoreType.DMA((2, STEPS, 2)),
             pltpu.SemaphoreType.DMA((2, STEPS, 2)),
             pltpu.SemaphoreType.DMA((6,)),
@@ -401,7 +411,28 @@
             collective_id=0, has_side_effects=True, vmem_limit_bytes=60 * 1024 * 1024
         ),
         name="inversion",
-    )(*args)
+    )(
+        velocity,
+        aperture_start,
+        aperture_count,
+        wave_prev,
+        wave_now,
+        adjoint_prev,
+        adjoint_now,
+        jnp.transpose(source_cells, (2, 0, 1)),
+        wavelet,
+        jnp.transpose(receiver_cells, (2, 0, 1)),
+        trace,
+    )
+    return pl.pallas_call(
+        deliver,
+        out_shape=out_shape,
+        in_specs=[pl.BlockSpec(memory_space=pltpu.VMEM)] * 3,
+        out_specs=(anywhere,) * 3,
+        scratch_shapes=[pltpu.SemaphoreType.DMA((3,))],
+        compiler_params=pltpu.CompilerParams(vmem_limit_bytes=1024 * 1024),
+        name="deliver",
+    )(*results)
 
 
 def solution(mesh):

time: 51.7 us -> 47.1 us (0.911)
  local copies, waits for them, and re-layouts: 4.57 us -> 0 us
    unnamed x13 -> x0, local copies, waits for them, and re-layouts: 4.57 us -> none
    pallas_call x1 -> x2, Pallas kernels: 44.9 us -> 45 us  [the longest x1 44.1 us: per_device(): pl.pallas_call(kernel, out_shape=tuple((pltpu.VMEM(leaf.shape, leaf.dtype...]
where the time goes in v2:
time: 47.1 us; the launch traced here: 46.9 us
  Pallas kernels  45 us (96%)
  between operations  1.93 us (4%)
    pallas_call x1, Pallas kernels, per_device(): pl.pallas_call(kernel, out_shape=tuple((pltpu.VMEM(leaf.shape, leaf.dtype...  44.1 us

profile of v2, /device:TPU:347, one launch (start us, length us, event | category | flops | bytes accessed | tf_op | source)
XLA Modules:
  0.0 46.9 jit_solution(7653980361524529905)
XLA Ops:
  1.9 44.1 %inversion.1 = (f32[1,16,32,128]{3,2,1,0:T(8,128)S(1)}, f32[1,16,32,128]{3,2,1,0:T(8,128)S(1)}, f32[16,8,128]{2,1,0:T(8,128)S(1)}) custom-call(f32[16,8,128]{2,1,0:T(8,128)} %velocity.1, s32[1]{0:T(128)S(6)} %copy.14.aperture_start, s32[1]{0:T(128)S(6)} %copy.15.aperture_count, f32[1,16,32,128]{3,2,1,0:T(8,128)} %wave_prev.1, f32[1,16,32,128]{3,2,1,0:T(8,128)} %wave_now.1, ...), custom_call_target="tpu_custom_call" | custom-call | tf_op jit(solution)/shard_map/inversion/pallas_call | solution.py:382
  46.1 0.8 %deliver.1 = (f32[1,16,32,128]{3,2,1,0:T(8,128)}, f32[1,16,32,128]{3,2,1,0:T(8,128)}, f32[16,8,128]{2,1,0:T(8,128)}) custom-call(f32[1,16,32,128]{3,2,1,0:T(8,128)S(1)} %get-tuple-element.6.refs_0_, f32[1,16,32,128]{3,2,1,0:T(8,128)S(1)} %get-tuple-element.7.refs_1_, f32[16,8,128]{2,1,0:T(8,128)S(1)} %get-tuple-element.8.refs_2_), custom_call_target="tpu_custom_call" | custom-call | tf_op jit(solution)/shard_map/deliver/pallas_call | solution.py:427

commit v3 on v2

--- a/solution.py
+++ b/solution.py
@@ -20,19 +20,25 @@
 
 def kernel(
     velocity,
-    aperture_start,
-    aperture_count,
+    aperture_start_in,
+    aperture_count_in,
     wave_prev,
     wave_now,
     adjoint_prev,
     adjoint_now,
+    source_cells_in,
+    wavelet_in,
+    receiver_cells_in,
+    trace_in,
+    wave_out,
+    adjoint_out,
+    gradient_out,
+    aperture_start,
+    aperture_count,
     source_cells,
     wavelet,
     receiver_cells,
     trace,
-    wave_out,
-    adjoint_out,
-    gradient_out,
     field,
     nearby,
     courant,
@@ -48,6 +54,7 @@
     to_pair,
     from_pair,
     load_sem,
+    table_sem,
     halo_send,
     halo_recv,
     block_send,
@@ -100,6 +107,19 @@
     ]
     for load in loads:
         load.start()
+    tables = [
+        pltpu.make_async_copy(table, held, table_sem.at[i])
+        for i, (table, held) in enumerate((
+            (aperture_start_in, aperture_start),
+            (aperture_count_in, aperture_count),
+            (source_cells_in, source_cells),
+            (wavelet_in, wavelet),
+            (receiver_cells_in, receiver_cells),
+            (trace_in, trace),
+        ))
+    ]
+    for table in tables:
+        table.start()
 
     def clear(edge):
         for f in range(2):
@@ -153,10 +173,10 @@
     sibling_high = remote(
         nearby.at[REACH + 2], nearby.at[shift + 2], block_send.at[5], block_recv.at[5], {"shot": sibling})
 
-    start_halos(0, 0)
     for send in (velocity_down, velocity_up, velocity_far):
         on(send[0], send[-1].start)
     sibling_own.start()
+    start_halos(0, 0)
     start_halos(1, 0)
 
     def clear_rows(i, carry):
@@ -167,6 +187,10 @@
         return carry
 
     lax.fori_loop(0, layers, clear_rows, 0)
+    for h in range(2):
+        for j in range(REACH):
+            spread[h, j] = jnp.zeros(spread.shape[2:], jnp.float32)
+            spread[h, REACH + blocks + j] = jnp.zeros(spread.shape[2:], jnp.float32)
 
     apart = jnp.abs(
         lax.broadcasted_iota(jnp.int32, (depth, depth), 0) - lax.broadcasted_iota(jnp.int32, (depth, depth), 1)
@@ -180,6 +204,8 @@
         depth_op[pl.ds(half * depth, depth), pl.ds(0, depth)] = op_high
         depth_op[pl.ds(half * depth, depth), pl.ds(depth, depth)] = op_low
 
+    for table in tables:
+        table.wait()
     at_y = lax.broadcasted_iota(jnp.int32, (PAD, depth), 0)
     at_z = lax.broadcasted_iota(jnp.int32, (PAD, depth), 1)
     first = slab * layers
@@ -264,84 +290,97 @@
     def edges(f, t):
         lax.fori_loop(0, 2, lambda b, c: (advance(f, t, b * (layers - BLOCK)), c)[1], 0)
 
-    grad_sibling = remote(to_sibling, from_sibling, grad_send.at[0], grad_recv.at[0], {"shot": sibling})
-    grad_far = (has_far, remote(to_far, from_far, grad_send.at[1], grad_recv.at[1], {"shot": far}))
-    grad_down = (has_down, has_up, remote(
-        to_pair.at[0], from_pair.at[1], grad_send.at[2], grad_recv.at[2], down))
-    grad_up = (has_up, has_down, remote(
-        to_pair.at[1], from_pair.at[0], grad_send.at[3], grad_recv.at[3], up))
+    parts = (((HALO, layers - 2 * HALO, 0),), ((0, HALO, 0), (layers - HALO, HALO, HALO)))
+
+    def grad_copies(h):
+        return (
+            remote(to_sibling.at[h], from_sibling.at[h], grad_send.at[h, 0], grad_recv.at[h, 0], {"shot": sibling}),
+            remote(to_far.at[h], from_far.at[h], grad_send.at[h, 1], grad_recv.at[h, 1], {"shot": far}),
+            remote(to_pair.at[h, 0], from_pair.at[h, 1], grad_send.at[h, 2], grad_recv.at[h, 2], down),
+            remote(to_pair.at[h, 1], from_pair.at[h, 0], grad_send.at[h, 3], grad_recv.at[h, 3], up),
+        )
+
+    grads = [grad_copies(h) for h in range(2)]
     back = 2 * REACH - offset
 
-    def piece(o):
-        return spread[back + o]
-
-    def send_gradient():
-        for j in range(REACH):
-            spread[j] = jnp.zeros(spread.shape[1:], jnp.float32)
-            spread[REACH + blocks + j] = jnp.zeros(spread.shape[1:], jnp.float32)
+    def piece(h, o):
+        return spread[h, back + o]
+
+    def send_gradient(h):
         for j in range(blocks):
             here = pl.ds(j * brows, brows)
-            spread[REACH + j] = grad[:, here, :] * imaging[:, here, :]
+            for start, size, at in parts[h]:
+                own = pl.ds(start, size)
+                spread[h, REACH + j, pl.ds(at, size)] = grad[own, here, :] * imaging[own, here, :]
         toward = 1 - 2 * core
         for i, o in enumerate((0, -2, 2)):
-            to_sibling[i] = piece(toward + o)
-        grad_sibling.start()
-        to_far[...] = piece(6 * core - 3)
-        on(has_far, grad_far[1].start)
-
-    def pass_gradient():
-        grad_sibling.wait_recv()
-        to_pair[0] = piece(-2) + from_sibling[1]
-        to_pair[1] = piece(2) + from_sibling[2]
-        on(has_down, grad_down[2].start)
-        on(has_up, grad_up[2].start)
-
-    def take_gradient():
-        total = piece(0) + from_sibling[0]
-        on(has_far, grad_far[1].wait_recv)
-        on(has_up, grad_down[2].wait_recv)
-        on(has_down, grad_up[2].wait_recv)
-        total = total + jnp.where(has_far, from_far[...], 0.0)
-        total = total + jnp.where(has_down, from_pair[0], 0.0)
-        total = total + jnp.where(has_up, from_pair[1], 0.0)
-        gradient_out[...] = total
+            to_sibling[h, i] = piece(h, toward + o)
+        grads[h][0].start()
+        to_far[h] = piece(h, 6 * core - 3)
+        on(has_far, grads[h][1].start)
+
+    def pass_gradient(h):
+        grads[h][0].wait_recv()
+        to_pair[h, 0] = piece(h, -2) + from_sibling[h, 1]
+        to_pair[h, 1] = piece(h, 2) + from_sibling[h, 2]
+        on(has_down, grads[h][2].start)
+        on(has_up, grads[h][3].start)
+
+    def take_gradient(h):
+        total = piece(h, 0) + from_sibling[h, 0]
+        on(has_far, grads[h][1].wait_recv)
+        on(has_up, grads[h][2].wait_recv)
+        on(has_down, grads[h][3].wait_recv)
+        total = total + jnp.where(has_far, from_far[h], 0.0)
+        total = total + jnp.where(has_down, from_pair[h, 0], 0.0)
+        total = total + jnp.where(has_up, from_pair[h, 1], 0.0)
+        for start, size, at in parts[h]:
+            gradient_out[pl.ds(start, size)] = total[at : at + size]
 
     def mask_halos(f):
         keep(f, 1, 0, HALO)
         keep(f, 1, HALO + layers, HALO)
 
-    for t in range(STEPS):
-        last = t == STEPS - 1
+    for t in range(STEPS - 1):
         inside(0, t)
         wait_halos(0, t)
         if t == 0:
             mask_halos(0)
         edges(0, t)
-        if last:
-            send_gradient()
-        else:
-            start_halos(0, t + 1)
+        start_halos(0, t + 1)
         inside(1, t)
-        if last:
-            pass_gradient()
         wait_halos(1, t)
         if t == 0:
             mask_halos(1)
         edges(1, t)
-        if not last:
-            start_halos(1, t + 1)
-    take_gradient()
+        start_halos(1, t + 1)
+
+    t = STEPS - 1
+    inside(0, t)
+    send_gradient(0)
+    inside(1, t)
+    wait_halos(0, t)
+    pass_gradient(0)
+    edges(0, t)
+    send_gradient(1)
+    pass_gradient(1)
+    wait_halos(1, t)
+    edges(1, t)
+    take_gradient(0)
+    take_gradient(1)
 
     for f in range(2):
         for t in range(STEPS):
             for to, _, copy in halos[f][t]:
                 on(to, copy.wait_send)
-    for send in (velocity_far, velocity_down, velocity_up, grad_far, grad_down, grad_up):
+    for send in (velocity_far, velocity_down, velocity_up):
         on(send[0], send[-1].wait_send)
+    for h in range(2):
+        for to, copy in zip((None, has_far, has_down, has_up), grads[h]):
+            on(to, copy.wait_send)
     sibling_own.wait_send()
     on(has_down, sibling_low.wait_send)
     on(has_up, sibling_high.wait_send)
-    grad_sibling.wait_send()
 
 
 def deliver(*refs):
@@ -371,8 +410,8 @@
     rows = wave_now.shape[2]
     blocks = rows // brows
     block = (layers, brows, depth)
+    half = (layers // 2, brows, depth)
     anywhere = pl.BlockSpec(memory_space=pl.ANY)
-    scalars = pl.BlockSpec(memory_space=pltpu.SMEM)
     f32 = jnp.float32
     out_shape = (
         jax.ShapeDtypeStruct(wave_now.shape, f32),
@@ -382,30 +421,37 @@
     results = pl.pallas_call(
         kernel,
         out_shape=tuple(pltpu.VMEM(leaf.shape, leaf.dtype) for leaf in out_shape),
-        in_specs=[anywhere, scalars, scalars] + [anywhere] * 4 + [scalars] * 4,
+        in_specs=[anywhere] * 11,
         out_specs=(pl.BlockSpec(memory_space=pltpu.VMEM),) * 3,
         scratch_shapes=[
+            pltpu.SMEM(aperture_start.shape, jnp.int32),
+            pltpu.SMEM(aperture_count.shape, jnp.int32),
+            pltpu.SMEM((3, 1, source_cells.shape[1]), jnp.int32),
+            pltpu.SMEM(wavelet.shape, f32),
+            pltpu.SMEM((3, 1, receiver_cells.shape[1]), jnp.int32),
+            pltpu.SMEM(trace.shape, f32),
             pltpu.VMEM((2, STEPS + 1, layers + 2 * HALO, rows + 2 * PAD, depth), f32),
             pltpu.VMEM((2 * REACH + 1, *block), f32),
             pltpu.VMEM((layers, rows, depth), f32),
             pltpu.VMEM((layers, rows, depth), f32),
             pltpu.VMEM((layers, rows, depth), f32),
-            pltpu.VMEM((blocks + 2 * REACH, *block), f32),
+            pltpu.VMEM((2, blocks + 2 * REACH, *half), f32),
             pltpu.VMEM((2, STEPS, layers, PAD, depth), f32),
             pltpu.VMEM((2 * depth, 2 * depth), jnp.bfloat16),
-            pltpu.VMEM((3, *block), f32),
-            pltpu.VMEM((3, *block), f32),
-            pltpu.VMEM(block, f32),
-            pltpu.VMEM(block, f32),
-            pltpu.VMEM((2, *block), f32),
-            pltpu.VMEM((2, *block), f32),
+            pltpu.VMEM((2, 3, *half), f32),
+            pltpu.VMEM((2, 3, *half), f32),
+            pltpu.VMEM((2, *half), f32),
+            pltpu.VMEM((2, *half), f32),
+            pltpu.VMEM((2, 2, *half), f32),
+            pltpu.VMEM((2, 2, *half), f32),
             pltpu.SemaphoreType.DMA((5,)),
+            pltpu.SemaphoreType.DMA((6,)),
             pltpu.SemaphoreType.DMA((2, STEPS, 2)),
             pltpu.SemaphoreType.DMA((2, STEPS, 2)),
             pltpu.SemaphoreType.DMA((6,)),
             pltpu.SemaphoreType.DMA((6,)),
-            pltpu.SemaphoreType.DMA((4,)),
-            pltpu.SemaphoreType.DMA((4,)),
+            pltpu.SemaphoreType.DMA((2, 4)),
+            pltpu.SemaphoreType.DMA((2, 4)),
         ],
         compiler_params=pltpu.CompilerParams(
             collective_id=0, has_side_effects=True, vmem_limit_bytes=60 * 1024 * 1024

time: 47.1 us -> 45.5 us (0.966)
  the two profiles are of different devices: /device:TPU:347 before, /device:TPU:411 now
where the time goes in v3:
time: 45.5 us; the launch traced here: 45.4 us
  Pallas kernels  43.4 us (95%)
  between operations  1.93 us (4%)
    pallas_call x1, Pallas kernels, per_device(): pl.pallas_call(kernel, out_shape=tuple((pltpu.VMEM(leaf.shape, leaf.dtype...  42.6 us

profile of v3, /device:TPU:411, one launch (start us, length us, event | category | flops | bytes accessed | tf_op | source)
XLA Modules:
  0.0 45.4 jit_solution(923721454404515698)
XLA Ops:
  1.9 42.6 %inversion.1 = (f32[1,16,32,128]{3,2,1,0:T(8,128)S(1)}, f32[1,16,32,128]{3,2,1,0:T(8,128)S(1)}, f32[16,8,128]{2,1,0:T(8,128)S(1)}) custom-call(f32[16,8,128]{2,1,0:T(8,128)} %velocity.1, s32[1]{0:T(128)S(6)} %copy.14.aperture_start_in, s32[1]{0:T(128)S(6)} %copy.15.aperture_count_in, f32[1,16,32,128]{3,2,1,0:T(8,128)} %wave_prev.1, ...), custom_call_target="tpu_custom_call" | custom-call | tf_op jit(solution)/shard_map/inversion/pallas_call | solution.py:421
  44.5 0.8 %deliver.1 = (f32[1,16,32,128]{3,2,1,0:T(8,128)}, f32[1,16,32,128]{3,2,1,0:T(8,128)}, f32[16,8,128]{2,1,0:T(8,128)}) custom-call(f32[1,16,32,128]{3,2,1,0:T(8,128)S(1)} %get-tuple-element.6.refs_0_, f32[1,16,32,128]{3,2,1,0:T(8,128)S(1)} %get-tuple-element.7.refs_1_, f32[16,8,128]{2,1,0:T(8,128)S(1)} %get-tuple-element.8.refs_2_), custom_call_target="tpu_custom_call" | custom-call | tf_op jit(solution)/shard_map/deliver/pallas_call | solution.py:473

commit v4 on v3

--- a/solution.py
+++ b/solution.py
@@ -40,7 +40,8 @@
     receiver_cells,
     trace,
     field,
-    nearby,
+    nearby_inner,
+    nearby_edges,
     courant,
     imaging,
     grad,
@@ -70,9 +71,15 @@
     core = lax.rem(shot, 2)
     sibling = shot + 1 - 2 * core
     far = shot - 3 + 6 * core
+    column = lax.rem(shot // 2, 2)
+    across = shot + 2 - 4 * column
+    onward, backward = shot + 4 - 8 * column, shot - 4 + 8 * column
+    beside = 1 - 2 * core
     has_left, has_right = slab > 0, slab < slabs - 1
     has_far = (far >= 0) & (far < shots)
     has_down, has_up = shot >= 2, shot < shots - 2
+    has_onward = (onward >= 0) & (onward < shots)
+    has_backward = (backward >= 0) & (backward < shots)
     inner = pl.ds(PAD, rows)
     mine = pl.ds(HALO, layers)
 
@@ -88,7 +95,10 @@
         (has_right, right),
         (has_down, down),
         (has_up, up),
-        (has_far, {"shot": far}),
+        (has_onward, {"shot": onward}),
+        (has_onward, {"shot": onward + beside}),
+        (has_backward, {"shot": backward}),
+        (has_backward, {"shot": backward + beside}),
         (None, {"shot": sibling}),
     )
 
@@ -98,12 +108,16 @@
         else:
             pl.when(condition)(action)
 
+    nearby = (nearby_inner, nearby_edges)
     loads = [
         pltpu.make_async_copy(wave_now.at[0], field.at[0, 1, mine, inner], load_sem.at[0]),
         pltpu.make_async_copy(adjoint_now.at[0], field.at[1, 1, mine, inner], load_sem.at[1]),
         pltpu.make_async_copy(wave_prev.at[0], field.at[0, 0, mine, inner], load_sem.at[2]),
         pltpu.make_async_copy(adjoint_prev.at[0], field.at[1, 0, mine, inner], load_sem.at[3]),
-        pltpu.make_async_copy(velocity, nearby.at[REACH], load_sem.at[4]),
+        pltpu.make_async_copy(velocity.at[pl.ds(HALO, layers - 2 * HALO)], nearby_inner.at[REACH], load_sem.at[4]),
+        pltpu.make_async_copy(velocity.at[pl.ds(0, HALO)], nearby_edges.at[REACH, pl.ds(0, HALO)], load_sem.at[5]),
+        pltpu.make_async_copy(
+            velocity.at[pl.ds(layers - HALO, HALO)], nearby_edges.at[REACH, pl.ds(HALO, HALO)], load_sem.at[6]),
     ]
     for load in loads:
         load.start()
@@ -156,28 +170,49 @@
         for to, _, copy in halos[f][t]:
             on(to, copy.start)
 
+    def sent_halos(f, t):
+        for to, _, copy in halos[f][t]:
+            on(to, copy.wait_send)
+
     def wait_halos(f, t):
         for _, given, copy in halos[f][t]:
             on(given, copy.wait_recv)
 
-    shift = 2 * core - 1 + REACH
-    velocity_far = (has_far, remote(
-        velocity, nearby.at[6 * (1 - core)], block_send.at[0], block_recv.at[0], {"shot": far}))
-    velocity_down = (has_down, has_up, remote(
-        velocity, nearby.at[REACH + 2], block_send.at[1], block_recv.at[1], down))
-    velocity_up = (has_up, has_down, remote(
-        velocity, nearby.at[REACH - 2], block_send.at[2], block_recv.at[2], up))
-    sibling_own = remote(velocity, nearby.at[shift], block_send.at[3], block_recv.at[3], {"shot": sibling})
-    sibling_low = remote(
-        nearby.at[REACH - 2], nearby.at[shift - 2], block_send.at[4], block_recv.at[4], {"shot": sibling})
-    sibling_high = remote(
-        nearby.at[REACH + 2], nearby.at[shift + 2], block_send.at[5], block_recv.at[5], {"shot": sibling})
-
-    for send in (velocity_down, velocity_up, velocity_far):
-        on(send[0], send[-1].start)
-    sibling_own.start()
+    entry = REACH + 2 - 4 * column
+
+    def block_copies(h):
+        def send(i, source, slot, where):
+            return remote(nearby[h].at[source], nearby[h].at[slot], block_send.at[h, i], block_recv.at[h, i], {"shot": where})
+
+        return (
+            (None, None, send(0, REACH, 2 * REACH - entry, across)),
+            (None, None, send(1, REACH, REACH - beside, sibling)),
+            (has_far, has_far, send(2, REACH, 6 * (1 - core), far)),
+            (None, None, send(3, entry, entry - beside, sibling)),
+            (has_onward, has_backward, send(4, entry, 2 * REACH - entry, onward)),
+            (has_onward, has_backward, send(5, entry, 2 * REACH - entry - beside, onward + beside)),
+        )
+
+    block_sends = [block_copies(h) for h in range(2)]
+
+    def send_blocks(h):
+        for i in range(3):
+            on(block_sends[h][i][0], block_sends[h][i][2].start)
+
+    def forward_blocks(h):
+        block_sends[h][0][2].wait_recv()
+        for i in (4, 5, 3):
+            on(block_sends[h][i][0], block_sends[h][i][2].start)
+
+    def wait_blocks(h):
+        for i in range(1, 6):
+            on(block_sends[h][i][1], block_sends[h][i][2].wait_recv)
+
+    for load in loads[4:]:
+        load.wait()
+    send_blocks(1)
     start_halos(0, 0)
-    start_halos(1, 0)
+    send_blocks(0)
 
     def clear_rows(i, carry):
         for f in range(2):
@@ -206,6 +241,22 @@
 
     for table in tables:
         table.wait()
+    live_rows = aperture_count[0] * brows
+    at_row = lax.broadcasted_iota(jnp.int32, (1, rows, depth), 1)
+    live = at_row < live_rows
+
+    def keep(f, t, start, size):
+        part = field[f, t, pl.ds(start, size), inner, :]
+        field[f, t, pl.ds(start, size), inner, :] = jnp.where(live, part, 0.0)
+
+    for i, (f, t) in enumerate(((0, 1), (1, 1), (0, 0), (1, 0))):
+        loads[i].wait()
+        lax.fori_loop(0, layers // BLOCK, lambda b, c, f=f, t=t: (keep(f, t, HALO + b * BLOCK, BLOCK), c)[1], 0)
+
+    forward_blocks(1)
+    sent_halos(0, 0)
+    start_halos(1, 0)
+
     at_y = lax.broadcasted_iota(jnp.int32, (PAD, depth), 0)
     at_z = lax.broadcasted_iota(jnp.int32, (PAD, depth), 1)
     first = slab * layers
@@ -226,36 +277,22 @@
 
         lax.fori_loop(0, layers, inject, 0)
 
-    live_rows = aperture_count[0] * brows
-    at_row = lax.broadcasted_iota(jnp.int32, (1, rows, depth), 1)
-    live = at_row < live_rows
-
-    def keep(f, t, start, size):
-        part = field[f, t, pl.ds(start, size), inner, :]
-        field[f, t, pl.ds(start, size), inner, :] = jnp.where(live, part, 0.0)
-
-    for i, (f, t) in enumerate(((0, 1), (1, 1), (0, 0), (1, 0))):
-        loads[i].wait()
-        lax.fori_loop(0, layers // BLOCK, lambda b, c, f=f, t=t: (keep(f, t, HALO + b * BLOCK, BLOCK), c)[1], 0)
-
-    on(velocity_down[1], velocity_down[2].wait_recv)
-    on(velocity_up[1], velocity_up[2].wait_recv)
-    on(has_down, sibling_low.start)
-    on(has_up, sibling_high.start)
-    loads[4].wait()
-    on(has_far, velocity_far[1].wait_recv)
-    sibling_own.wait_recv()
-    sib_down, sib_up = sibling >= 2, sibling < shots - 2
-    on(sib_down, sibling_low.wait_recv)
-    on(sib_up, sibling_high.wait_recv)
+    forward_blocks(0)
 
     offset = jnp.clip(aperture_start[0] - shot + REACH, 0, REACH)
-    for j in range(blocks):
-        part = nearby[offset + j]
-        here = pl.ds(j * brows, brows)
-        alive = j * brows < live_rows
-        imaging[:, here, :] = part * jnp.float32(2.0 * time_step * time_step)
-        courant[:, here, :] = jnp.where(alive, part * part * jnp.float32(time_step * time_step), 0.0)
+    parts = (((HALO, layers - 2 * HALO, 0),), ((0, HALO, 0), (layers - HALO, HALO, HALO)))
+
+    def lay_window(h):
+        wait_blocks(h)
+        for j in range(blocks):
+            here = pl.ds(j * brows, brows)
+            alive = j * brows < live_rows
+            for start, size, at in parts[h]:
+                part = nearby[h][offset + j, pl.ds(at, size)]
+                imaging[pl.ds(start, size), here, :] = part * jnp.float32(2.0 * time_step * time_step)
+                courant[pl.ds(start, size), here, :] = jnp.where(
+                    alive, part * part * jnp.float32(time_step * time_step), 0.0
+                )
 
     def advance(f, t, x):
         here = pl.ds(HALO + x, BLOCK)
@@ -290,8 +327,6 @@
     def edges(f, t):
         lax.fori_loop(0, 2, lambda b, c: (advance(f, t, b * (layers - BLOCK)), c)[1], 0)
 
-    parts = (((HALO, layers - 2 * HALO, 0),), ((0, HALO, 0), (layers - HALO, HALO, HALO)))
-
     def grad_copies(h):
         return (
             remote(to_sibling.at[h], from_sibling.at[h], grad_send.at[h, 0], grad_recv.at[h, 0], {"shot": sibling}),
@@ -341,19 +376,27 @@
         keep(f, 1, 0, HALO)
         keep(f, 1, HALO + layers, HALO)
 
-    for t in range(STEPS - 1):
-        inside(0, t)
-        wait_halos(0, t)
-        if t == 0:
-            mask_halos(0)
-        edges(0, t)
-        start_halos(0, t + 1)
-        inside(1, t)
-        wait_halos(1, t)
-        if t == 0:
-            mask_halos(1)
-        edges(1, t)
-        start_halos(1, t + 1)
+    lay_window(1)
+    for f in range(2):
+        wait_halos(f, 0)
+        mask_halos(f)
+        edges(f, 0)
+        if f:
+            sent_halos(0, 1)
+        else:
+            sent_halos(1, 0)
+        start_halos(f, 1)
+    lay_window(0)
+    inside(0, 0)
+    inside(1, 0)
+
+    for t in range(1, STEPS - 1):
+        for f in range(2):
+            inside(f, t)
+            wait_halos(f, t)
+            edges(f, t)
+            sent_halos(1 - f, t + f)
+            start_halos(f, t + 1)
 
     t = STEPS - 1
     inside(0, t)
@@ -369,18 +412,13 @@
     take_gradient(0)
     take_gradient(1)
 
-    for f in range(2):
-        for t in range(STEPS):
-            for to, _, copy in halos[f][t]:
-                on(to, copy.wait_send)
-    for send in (velocity_far, velocity_down, velocity_up):
-        on(send[0], send[-1].wait_send)
+    sent_halos(1, STEPS - 1)
+    for h in range(2):
+        for to, _, copy in block_sends[h]:
+            on(to, copy.wait_send)
     for h in range(2):
         for to, copy in zip((None, has_far, has_down, has_up), grads[h]):
             on(to, copy.wait_send)
-    sibling_own.wait_send()
-    on(has_down, sibling_low.wait_send)
-    on(has_up, sibling_high.wait_send)
 
 
 def deliver(*refs):
@@ -431,7 +469,8 @@
             pltpu.SMEM((3, 1, receiver_cells.shape[1]), jnp.int32),
             pltpu.SMEM(trace.shape, f32),
             pltpu.VMEM((2, STEPS + 1, layers + 2 * HALO, rows + 2 * PAD, depth), f32),
-            pltpu.VMEM((2 * REACH + 1, *block), f32),
+            pltpu.VMEM((2 * REACH + 1, *half), f32),
+            pltpu.VMEM((2 * REACH + 1, *half), f32),
             pltpu.VMEM((layers, rows, depth), f32),
             pltpu.VMEM((layers, rows, depth), f32),
             pltpu.VMEM((layers, rows, depth), f32),
@@ -444,12 +483,12 @@
             pltpu.VMEM((2, *half), f32),
             pltpu.VMEM((2, 2, *half), f32),
             pltpu.VMEM((2, 2, *half), f32),
-            pltpu.SemaphoreType.DMA((5,)),
+            pltpu.SemaphoreType.DMA((7,)),
             pltpu.SemaphoreType.DMA((6,)),
             pltpu.SemaphoreType.DMA((2, STEPS, 2)),
             pltpu.SemaphoreType.DMA((2, STEPS, 2)),
-            pltpu.SemaphoreType.DMA((6,)),
-            pltpu.SemaphoreType.DMA((6,)),
+            pltpu.SemaphoreType.DMA((2, 6)),
+            pltpu.SemaphoreType.DMA((2, 6)),
             pltpu.SemaphoreType.DMA((2, 4)),
             pltpu.SemaphoreType.DMA((2, 4)),
         ],

time: 45.5 us -> 43.9 us (0.965)
  the two profiles are of different devices: /device:TPU:411 before, /device:TPU:221 now
where the time goes in v4:
time: 43.9 us; the launch traced here: 43.8 us
  Pallas kernels  41.8 us (95%)
  between operations  1.93 us (4%)
    pallas_call x1, Pallas kernels, per_device(): pl.pallas_call(kernel, out_shape=tuple((pltpu.VMEM(leaf.shape, leaf.dtype...  41 us

profile of v4, /device:TPU:221, one launch (start us, length us, event | category | flops | bytes accessed | tf_op | source)
XLA Modules:
  0.0 43.8 jit_solution(13713235824337390077)
XLA Ops:
  1.9 41.0 %inversion.1 = (f32[1,16,32,128]{3,2,1,0:T(8,128)S(1)}, f32[1,16,32,128]{3,2,1,0:T(8,128)S(1)}, f32[16,8,128]{2,1,0:T(8,128)S(1)}) custom-call(f32[16,8,128]{2,1,0:T(8,128)} %velocity.1, s32[1]{0:T(128)S(6)} %copy.14.aperture_start_in, s32[1]{0:T(128)S(6)} %copy.15.aperture_count_in, f32[1,16,32,128]{3,2,1,0:T(8,128)} %wave_prev.1, ...), custom_call_target="tpu_custom_call" | custom-call | tf_op jit(solution)/shard_map/inversion/pallas_call | solution.py:459
  42.9 0.8 %deliver.1 = (f32[1,16,32,128]{3,2,1,0:T(8,128)}, f32[1,16,32,128]{3,2,1,0:T(8,128)}, f32[16,8,128]{2,1,0:T(8,128)}) custom-call(f32[1,16,32,128]{3,2,1,0:T(8,128)S(1)} %get-tuple-element.6.refs_0_, f32[1,16,32,128]{3,2,1,0:T(8,128)S(1)} %get-tuple-element.7.refs_1_, f32[16,8,128]{2,1,0:T(8,128)S(1)} %get-tuple-element.8.refs_2_), custom_call_target="tpu_custom_call" | custom-call | tf_op jit(solution)/shard_map/deliver/pallas_call | solution.py:512

commit v5 on v4

--- a/solution.py
+++ b/solution.py
@@ -212,7 +212,6 @@
         load.wait()
     send_blocks(1)
     start_halos(0, 0)
-    send_blocks(0)
 
     def clear_rows(i, carry):
         for f in range(2):
@@ -239,6 +238,8 @@
         depth_op[pl.ds(half * depth, depth), pl.ds(0, depth)] = op_high
         depth_op[pl.ds(half * depth, depth), pl.ds(depth, depth)] = op_low
 
+    forward_blocks(1)
+
     for table in tables:
         table.wait()
     live_rows = aperture_count[0] * brows
@@ -253,7 +254,7 @@
         loads[i].wait()
         lax.fori_loop(0, layers // BLOCK, lambda b, c, f=f, t=t: (keep(f, t, HALO + b * BLOCK, BLOCK), c)[1], 0)
 
-    forward_blocks(1)
+    send_blocks(0)
     sent_halos(0, 0)
     start_halos(1, 0)
 
@@ -383,8 +384,6 @@
         edges(f, 0)
         if f:
             sent_halos(0, 1)
-        else:
-            sent_halos(1, 0)
         start_halos(f, 1)
     lay_window(0)
     inside(0, 0)
@@ -395,7 +394,8 @@
             inside(f, t)
             wait_halos(f, t)
             edges(f, t)
-            sent_halos(1 - f, t + f)
+            if f:
+                sent_halos(0, t + 1)
             start_halos(f, t + 1)
 
     t = STEPS - 1
@@ -412,7 +412,8 @@
     take_gradient(0)
     take_gradient(1)
 
-    sent_halos(1, STEPS - 1)
+    for t in range(STEPS):
+        sent_halos(1, t)
     for h in range(2):
         for to, _, copy in block_sends[h]:
             on(to, copy.wait_send)

time: 43.9 us -> 43.1 us (0.982)
  the two profiles are of different devices: /device:TPU:221 before, /device:TPU:219 now
where the time goes in v5:
time: 43.1 us; the launch traced here: 43 us
  Pallas kernels  41 us (95%)
  between operations  1.93 us (4%)
    pallas_call x1, Pallas kernels, per_device(): pl.pallas_call(kernel, out_shape=tuple((pltpu.VMEM(leaf.shape, leaf.dtype...  40.2 us

profile of v5, /device:TPU:219, one launch (start us, length us, event | category | flops | bytes accessed | tf_op | source)
XLA Modules:
  0.0 43.0 jit_solution(14570266643649701375)
XLA Ops:
  1.9 40.2 %inversion.1 = (f32[1,16,32,128]{3,2,1,0:T(8,128)S(1)}, f32[1,16,32,128]{3,2,1,0:T(8,128)S(1)}, f32[16,8,128]{2,1,0:T(8,128)S(1)}) custom-call(f32[16,8,128]{2,1,0:T(8,128)} %velocity.1, s32[1]{0:T(128)S(6)} %copy.14.aperture_start_in, s32[1]{0:T(128)S(6)} %copy.15.aperture_count_in, f32[1,16,32,128]{3,2,1,0:T(8,128)} %wave_prev.1, ...), custom_call_target="tpu_custom_call" | custom-call | tf_op jit(solution)/shard_map/inversion/pallas_call | solution.py:460
  42.1 0.8 %deliver.1 = (f32[1,16,32,128]{3,2,1,0:T(8,128)}, f32[1,16,32,128]{3,2,1,0:T(8,128)}, f32[16,8,128]{2,1,0:T(8,128)}) custom-call(f32[1,16,32,128]{3,2,1,0:T(8,128)S(1)} %get-tuple-element.6.refs_0_, f32[1,16,32,128]{3,2,1,0:T(8,128)S(1)} %get-tuple-element.7.refs_1_, f32[16,8,128]{2,1,0:T(8,128)S(1)} %get-tuple-element.8.refs_2_), custom_call_target="tpu_custom_call" | custom-call | tf_op jit(solution)/shard_map/deliver/pallas_call | solution.py:513

commit v6 on v5

--- a/solution.py
+++ b/solution.py
@@ -255,7 +255,6 @@
         lax.fori_loop(0, layers // BLOCK, lambda b, c, f=f, t=t: (keep(f, t, HALO + b * BLOCK, BLOCK), c)[1], 0)
 
     send_blocks(0)
-    sent_halos(0, 0)
     start_halos(1, 0)
 
     at_y = lax.broadcasted_iota(jnp.int32, (PAD, depth), 0)
@@ -412,6 +411,7 @@
     take_gradient(0)
     take_gradient(1)
 
+    sent_halos(0, 0)
     for t in range(STEPS):
         sent_halos(1, t)
     for h in range(2):

time: 43.1 us -> 43.2 us (level)
  the two profiles are of different devices: /device:TPU:219 before, /device:TPU:223 now
where the time goes in v6:
time: 43.2 us; the launch traced here: 43 us
  Pallas kernels  41.1 us (95%)
  between operations  1.93 us (4%)
    pallas_call x1, Pallas kernels, per_device(): pl.pallas_call(kernel, out_shape=tuple((pltpu.VMEM(leaf.shape, leaf.dtype...  40.3 us

profile of v6, /device:TPU:223, one launch (start us, length us, event | category | flops | bytes accessed | tf_op | source)
XLA Modules:
  0.0 43.0 jit_solution(7750338790937716872)
XLA Ops:
  1.9 40.3 %inversion.1 = (f32[1,16,32,128]{3,2,1,0:T(8,128)S(1)}, f32[1,16,32,128]{3,2,1,0:T(8,128)S(1)}, f32[16,8,128]{2,1,0:T(8,128)S(1)}) custom-call(f32[16,8,128]{2,1,0:T(8,128)} %velocity.1, s32[1]{0:T(128)S(6)} %copy.14.aperture_start_in, s32[1]{0:T(128)S(6)} %copy.15.aperture_count_in, f32[1,16,32,128]{3,2,1,0:T(8,128)} %wave_prev.1, ...), custom_call_target="tpu_custom_call" | custom-call | tf_op jit(solution)/shard_map/inversion/pallas_call | solution.py:460
  42.2 0.8 %deliver.1 = (f32[1,16,32,128]{3,2,1,0:T(8,128)}, f32[1,16,32,128]{3,2,1,0:T(8,128)}, f32[16,8,128]{2,1,0:T(8,128)}) custom-call(f32[1,16,32,128]{3,2,1,0:T(8,128)S(1)} %get-tuple-element.6.refs_0_, f32[1,16,32,128]{3,2,1,0:T(8,128)S(1)} %get-tuple-element.7.refs_1_, f32[16,8,128]{2,1,0:T(8,128)S(1)} %get-tuple-element.8.refs_2_), custom_call_target="tpu_custom_call" | custom-call | tf_op jit(solution)/shard_map/deliver/pallas_call | solution.py:513
